TPU v7x, 256 devices: a whole 4x4x8 slice. The times are simulated.
256 devices in a mesh: row: 4 (over x), col: 64 (over y, z, core).
Axes of the slice: x: 4, y: 4, z: 8, core: 2. Of those that a mesh axis runs over, the one named last changes fastest.
Arguments:
- left_image: float32 [256, 16384], P('row', 'col'), may hold values from -6 to 6
- right_image: float32 [256, 16384], P('row', 'col'), may hold values from -6 to 6
Outputs:
- aggregated: float32 [256, 16384, 128], P('row', 'col')
All inputs are finite; a program needn't handle non-finite values.
Results may differ from a plain program's by a relative error of at most 0.0003.
Values sent between devices are 32-bit elements; how exact they have to be, the bound alone decides.
No kernel may reach another device: no remote copies, remote signals or barrier semaphores. Data moves between devices by JAX's collectives and lax.ppermute only.
A program may use at most 128 MiB of HBM per device.

v0:
```python
import jax
import jax.numpy as jnp
from jax import lax
from jax.sharding import PartitionSpec as P

ND = 128


def shifted(block, axis, distance):
    devices = range(lax.axis_size(axis))
    route = [(i - distance, i) for i in devices if i - distance in devices]
    return lax.ppermute(block, axis, route)


def extended(value, sides, width):
    for axis, dim in sides:
        peers, length = (lax.axis_size(axis), value.shape[dim])
        up = [(i, (i + 1) % peers) for i in range(peers - 1)]
        down = [(j, i) for i, j in up]
        last = lax.slice_in_dim(value, length - width, length, axis=dim)
        first = lax.slice_in_dim(value, 0, width, axis=dim)
        before = lax.ppermute(last, axis, up)
        after = lax.ppermute(first, axis, down)
        value = jnp.concatenate([before, value, after], axis=dim)
    return value


def reach(tile):
    pieces = []
    pieces.append(shifted(tile, "col", 1))
    pieces.append(tile)
    return jnp.concatenate(pieces, axis=1)


def shifted_slices(spread, first, count):
    return jnp.stack(
        [spread[:, first - disp : first - disp + count] for disp in range(ND)], axis=-1
    )


def window_rows(padded, count):
    summed = padded[0:count]
    for offset in range(1, 9):
        summed = summed + padded[offset : offset + count]
    return summed


def window_cols(padded, count):
    summed = padded[:, 0:count]
    for offset in range(1, 9):
        summed = summed + padded[:, offset : offset + count]
    return summed


def per_device(left_image, right_image):
    rows, width = left_image.shape
    tiles_left = (ND + 3 + width - 1) // width
    spread = reach(right_image)
    costs = jnp.abs(left_image[:, :, None] - shifted_slices(spread, tiles_left * width, width))
    padded = extended(costs, (("row", 0),), 4)
    summed = window_rows(padded, rows)
    padded = extended(summed, (("col", 1),), 4)
    total = window_cols(padded, width)
    return total / 81.0


def solution(mesh):
    in_specs = (P("row", "col"), P("row", "col"))
    out_specs = P("row", "col", None)
    return jax.shard_map(
        per_device, mesh=mesh, in_specs=in_specs, out_specs=out_specs, check_vma=False
    )
```

profile of v0, /device:TPU:27, one launch (start us, length us, event | category | flops | bytes accessed | tf_op | source)
XLA Modules:
  0.0 173.0 jit_solution(10852155775575172435)
XLA Ops:
  0.0 4.1 %collective-permute-start = (f32[64,256]{1,0:T(8,128)}, f32[64,256]{1,0:T(8,128)S(1)}, u32[]{:S(2)}, u32[]{:S(2)}) collective-permute-start(f32[64,256]{1,0:T(8,128)} %param.3), channel_id=1, source_target_pairs={{0,1},{1,2},{2,3},{3,4},{4,5},{5,6},{6,7},{7,8},{8,9},{9,10},{10,1... | collective-permute-start | bytes 196616 | tf_op jit(solution)/shard_map/ppermute | solution.py:12
  4.1 0.9 constant_dynamic-update-slice_fusion.129
  5.0 0.8 collective-permute-done
  5.7 0.9 constant_dynamic-update-slice_fusion
  6.8 0.1 constant_dynamic-update-slice_fusion.126
  6.9 0.1 constant_dynamic-update-slice_fusion.125
  7.0 0.1 constant_dynamic-update-slice_fusion.124
  17.6 1.9 %subtract_abs_fusion = f32[64,256,128]{1,0,2:T(8,128)S(1)} fusion(f32[64,256,128]{1,0,2:T(8,128)S(1)} %constant_dynamic-update-slice_fusion.2, f32[64,256]{1,0:T(8,128)S(1)} %copy-done.2), kind=kLoop, calls=%fused_computation.57 | loop fusion | flops 4194304 | bytes 16842752 | tf_op jit(solution)/shard_map/abs | solution.py:59
  19.6 0.2 fusion.30
  19.8 3.1 %collective-permute-start.1 = (f32[4,256,128]{1,0,2:T(4,128)S(1)}, f32[4,256,128]{1,0,2:T(4,128)S(1)}, u32[]{:S(2)}, u32[]{:S(2)}) collective-permute-start(f32[4,256,128]{1,0,2:T(4,128)S(1)} %get-tuple-element.7), channel_id=1, source_target_pairs={{0,64},{64,128},{128,192},{1,65},{65,129},{129,193},{2,66},{66,130... | collective-permute-start | bytes 1572872 | tf_op jit(solution)/shard_map/ppermute | solution.py:22
  22.9 2.2 %collective-permute-start.2 = (f32[4,256,128]{1,0,2:T(4,128)S(1)}, f32[4,256,128]{1,0,2:T(4,128)S(1)}, u32[]{:S(2)}, u32[]{:S(2)}) collective-permute-start(f32[4,256,128]{1,0,2:T(4,128)S(1)} %get-tuple-element.8), channel_id=1, source_target_pairs={{64,0},{128,64},{192,128},{65,1},{129,65},{193,129},{66,2},{130,66... | collective-permute-start | bytes 1572872 | tf_op jit(solution)/shard_map/ppermute | solution.py:23
  25.1 5.5 %collective-permute-done.1 = f32[4,256,128]{1,0,2:T(4,128)S(1)} collective-permute-done((f32[4,256,128]{1,0,2:T(4,128)S(1)}, f32[4,256,128]{1,0,2:T(4,128)S(1)}, u32[]{:S(2)}, u32[]{:S(2)}) %collective-permute-start.1) | collective-permute-done | bytes 524320 | tf_op jit(solution)/shard_map/ppermute | solution.py:22
  30.6 2.8 %collective-permute-done.2 = f32[4,256,128]{1,0,2:T(4,128)S(1)} collective-permute-done((f32[4,256,128]{1,0,2:T(4,128)S(1)}, f32[4,256,128]{1,0,2:T(4,128)S(1)}, u32[]{:S(2)}, u32[]{:S(2)}) %collective-permute-start.2) | collective-permute-done | bytes 524320 | tf_op jit(solution)/shard_map/ppermute | solution.py:23
  33.4 34.5 %fusion.2 = f32[64,256,128]{1,0,2:T(8,128)S(1)} fusion(f32[64,256,128]{1,0,2:T(8,128)} %copy-done.1, f32[4,256,128]{1,0,2:T(4,128)S(1)} %collective-permute-done.2, f32[4,256,128]{1,0,2:T(4,128)S(1)} %collective-permute-done.1), kind=kLoop, calls=%fused_computation.26 | loop fusion | flops 33554432 | bytes 17825792 | tf_op jit(solution)/shard_map/add | solution.py:44
  68.0 3.4 %copy-done = f32[64,256,128]{1,0,2:T(8,128)} copy-done((f32[64,256,128]{1,0,2:T(8,128)}, f32[64,256,128]{1,0,2:T(8,128)S(1)}, u32[]{:S(2)}) %copy-start) | copy-done | bytes 8388632
  71.4 4.7 %fusion.29 = (f32[64,4,128]{1,0,2:T(8,128)}, f32[64,4,128]{1,0,2:T(8,128)}) fusion(f32[64,256,128]{1,0,2:T(8,128)S(1)} %fusion.2), kind=kLoop, calls=%fused_computation.315 | loop fusion | bytes 524288 | tf_op jit(solution)/shard_map/slice | solution.py:20
  76.1 3.7 %copy.130 = f32[64,4,128]{2,0,1:T(8,128)S(1)} copy(f32[64,4,128]{1,0,2:T(8,128)} %get-tuple-element.5) | data formatting | bytes 262144 | tf_op jit(solution)/shard_map/slice | solution.py:20
  79.8 9.1 %collective-permute-start.3 = (f32[64,4,128]{2,0,1:T(8,128)S(1)}, f32[64,4,128]{2,0,1:T(8,128)S(1)}, u32[]{:S(2)}, u32[]{:S(2)}) collective-permute-start(f32[64,4,128]{2,0,1:T(8,128)S(1)} %copy.130), channel_id=1, source_target_pairs={{0,1},{1,2},{2,3},{3,4},{4,5},{5,6},{6,7},{7,8},{8,9},{9,10},{10,1... | collective-permute-start | bytes 393224 | tf_op jit(solution)/shard_map/ppermute | solution.py:22
  88.9 3.8 %copy.132 = f32[64,4,128]{2,0,1:T(8,128)S(1)} copy(f32[64,4,128]{1,0,2:T(8,128)} %get-tuple-element.6) | data formatting | bytes 262144 | tf_op jit(solution)/shard_map/slice | solution.py:21
  92.7 2.1 %collective-permute-start.4 = (f32[64,4,128]{2,0,1:T(8,128)S(1)}, f32[64,4,128]{2,0,1:T(8,128)S(1)}, u32[]{:S(2)}, u32[]{:S(2)}) collective-permute-start(f32[64,4,128]{2,0,1:T(8,128)S(1)} %copy.132), channel_id=1, source_target_pairs={{1,0},{2,1},{3,2},{4,3},{5,4},{6,5},{7,6},{8,7},{9,8},{10,9},{11,1... | collective-permute-start | bytes 393224 | tf_op jit(solution)/shard_map/ppermute | solution.py:23
  94.8 4.5 %copy.131 = f32[64,4,128]{1,0,2:T(8,128)} copy(f32[64,4,128]{2,0,1:T(8,128)S(1)} %collective-permute-done.3) | data formatting | bytes 262144 | tf_op jit(solution)/shard_map/ppermute | solution.py:22
  99.3 4.5 %copy.133 = f32[64,4,128]{1,0,2:T(8,128)} copy(f32[64,4,128]{2,0,1:T(8,128)S(1)} %collective-permute-done.4) | data formatting | bytes 262144 | tf_op jit(solution)/shard_map/ppermute | solution.py:23
  103.8 59.9 %fusion.17 = f32[64,256,128]{1,0,2:T(8,128)} fusion(f32[64,256,128]{1,0,2:T(8,128)} %copy-done, f32[64,4,128]{1,0,2:T(8,128)} %copy.133, f32[64,4,128]{1,0,2:T(8,128)} %copy.131), kind=kLoop, calls=%fused_computation.41 | loop fusion | flops 35651584 | bytes 17039360 | tf_op jit(solution)/shard_map/div | solution.py:64
  163.7 9.3 %copy.134 = f32[64,256,128]{2,1,0:T(8,128)} copy(f32[64,256,128]{1,0,2:T(8,128)} %fusion.17) | data formatting | bytes 16777216 | tf_op jit(solution)/shard_map/div | solution.py:64
  (132 shorter events, 10.7 us)
Async XLA Ops:
  0.0 5.7 %collective-permute-start = (f32[64,256]{1,0:T(8,128)}, f32[64,256]{1,0:T(8,128)S(1)}, u32[]{:S(2)}, u32[]{:S(2)}) collective-permute-start(f32[64,256]{1,0:T(8,128)} %param.3), channel_id=1, source_target_pairs={{0,1},{1,2},{2,3},{3,4},{4,5},{5,6},{6,7},{7,8},{8,9},{9,10},{10,1... | collective-permute-start | bytes 196616 | tf_op jit(solution)/shard_map/ppermute | solution.py:12
  5.7 11.9 %copy-start.2 = (f32[64,256]{1,0:T(8,128)S(1)}, f32[64,256]{1,0:T(8,128)}, u32[]{:S(2)}) copy-start(f32[64,256]{1,0:T(8,128)} %param.2) | copy-start | bytes 196612
  19.6 11.0 %copy-start.1 = (f32[64,256,128]{1,0,2:T(8,128)}, f32[64,256,128]{1,0,2:T(8,128)S(1)}, u32[]{:S(2)}) copy-start(f32[64,256,128]{1,0,2:T(8,128)S(1)} %subtract_abs_fusion) | copy-start | bytes 25165828
  19.8 10.8 %collective-permute-start.1 = (f32[4,256,128]{1,0,2:T(4,128)S(1)}, f32[4,256,128]{1,0,2:T(4,128)S(1)}, u32[]{:S(2)}, u32[]{:S(2)}) collective-permute-start(f32[4,256,128]{1,0,2:T(4,128)S(1)} %get-tuple-element.7), channel_id=1, source_target_pairs={{0,64},{64,128},{128,192},{1,65},{65,129},{129,193},{2,66},{66,130... | collective-permute-start | bytes 1572872 | tf_op jit(solution)/shard_map/ppermute | solution.py:22
  22.9 10.5 %collective-permute-start.2 = (f32[4,256,128]{1,0,2:T(4,128)S(1)}, f32[4,256,128]{1,0,2:T(4,128)S(1)}, u32[]{:S(2)}, u32[]{:S(2)}) collective-permute-start(f32[4,256,128]{1,0,2:T(4,128)S(1)} %get-tuple-element.8), channel_id=1, source_target_pairs={{64,0},{128,64},{192,128},{65,1},{129,65},{193,129},{66,2},{130,66... | collective-permute-start | bytes 1572872 | tf_op jit(solution)/shard_map/ppermute | solution.py:23
  68.0 3.4 %copy-start = (f32[64,256,128]{1,0,2:T(8,128)}, f32[64,256,128]{1,0,2:T(8,128)S(1)}, u32[]{:S(2)}) copy-start(f32[64,256,128]{1,0,2:T(8,128)S(1)} %fusion.2) | copy-start | bytes 25165828
  79.8 15.0 %collective-permute-start.3 = (f32[64,4,128]{2,0,1:T(8,128)S(1)}, f32[64,4,128]{2,0,1:T(8,128)S(1)}, u32[]{:S(2)}, u32[]{:S(2)}) collective-permute-start(f32[64,4,128]{2,0,1:T(8,128)S(1)} %copy.130), channel_id=1, source_target_pairs={{0,1},{1,2},{2,3},{3,4},{4,5},{5,6},{6,7},{7,8},{8,9},{9,10},{10,1... | collective-permute-start | bytes 393224 | tf_op jit(solution)/shard_map/ppermute | solution.py:22
  92.7 6.6 %collective-permute-start.4 = (f32[64,4,128]{2,0,1:T(8,128)S(1)}, f32[64,4,128]{2,0,1:T(8,128)S(1)}, u32[]{:S(2)}, u32[]{:S(2)}) collective-permute-start(f32[64,4,128]{2,0,1:T(8,128)S(1)} %copy.132), channel_id=1, source_target_pairs={{1,0},{2,1},{3,2},{4,3},{5,4},{6,5},{7,6},{8,7},{9,8},{10,9},{11,1... | collective-permute-start | bytes 393224 | tf_op jit(solution)/shard_map/ppermute | solution.py:23
where the time goes:
time: 175 us; the launch traced here: 173 us
  other arithmetic  96.3 us (55%)
  local copies, waits for them, and re-layouts  46.7 us (27%)
  starting transfers between devices  20.6 us (12%)
  waiting for transfers between devices  9.12 us (5%)
    div x1, other arithmetic, per_device(): return total / 81.0  59.9 us
    add x1, other arithmetic, window_rows(): summed = summed + padded[offset:offset + count]  34.5 us
    unnamed x134, local copies, waits for them, and re-layouts  15.1 us
    ppermute x2, starting transfers between devices, extended(): before = lax.ppermute(last, axis, up)  12.2 us
    div x1, local copies, waits for them, and re-layouts, per_device(): return total / 81.0  9.26 us
    slice x3, local copies, waits for them, and re-layouts, extended(): last = lax.slice_in_dim(value, length - width, length, axis=dim)  8.62 us
    ppermute x2, waiting for transfers between devices, extended(): before = lax.ppermute(last, axis, up)  5.5 us
    ppermute x1, local copies, waits for them, and re-layouts, extended(): after = lax.ppermute(first, axis, down)  4.49 us
  transfers between devices with their start and end apart: 5, of which 3 were waited for; matrix products, arithmetic and copies ran while one was open for 5% of the time, Pallas kernels for 0%

commit v1 on v0

v1 whole, which is shorter than its diff:
```python
import functools

import jax
import jax.numpy as jnp
from jax import lax
from jax.experimental import pallas as pl
from jax.experimental.pallas import tpu as pltpu
from jax.sharding import PartitionSpec as P

ND = 128
ROWS = 64
COLS = 256
F32 = jnp.float32
BF16 = jnp.bfloat16
NT = (((1,), (1,)), ((), ()))
SCALE = 1.0 / 81.0
GROUP = 32
VMEM = pl.BlockSpec(memory_space=pltpu.VMEM)
HBM = pl.BlockSpec(memory_space=pl.ANY)


def iota(shape, dim):
    return lax.broadcasted_iota(jnp.int32, shape, dim)


def tile(ref, t):
    return ref[:, 128 * t : 128 * t + 128]


def one_hot(mask):
    return jnp.where(mask, 1.0, 0.0).astype(BF16)


def halves(x):
    high = x.astype(BF16)
    low = (x - high.astype(F32)).astype(BF16)
    return jnp.concatenate([high, low], axis=1)


def pick_transposed(chosen, x):
    a = x.astype(BF16)
    rest = x - a.astype(F32)
    b = rest.astype(BF16)
    c = (rest - b.astype(F32)).astype(BF16)
    dot = functools.partial(lax.dot_general, dimension_numbers=NT, preferred_element_type=F32)
    return (dot(chosen, c) + dot(chosen, b)) + dot(chosen, a)


def side_tiles(cross, intra):
    c = lax.axis_index("col")
    odd = (c % 2) == 1
    west = jnp.where(odd, intra, cross)
    east = jnp.where(odd, cross, intra)
    west = jnp.where(c == 0, 0.0, west)
    east = jnp.where(c == lax.axis_size("col") - 1, 0.0, east)
    lane = iota((west.shape[0], 128), 1)
    right_far = west[:, 0:128]
    right_edge = jnp.where(lane < 4, east[:, 128:256], west[:, 128:256])
    left_edge = pltpu.roll(jnp.where(lane >= 8, east[:, 128:256], west[:, 128:256]), 120, 1)
    return right_far, right_edge, left_edge


def pack_kernel(left, right, out):
    lane = iota((ROWS, 128), 1)
    edge = pltpu.roll(jnp.where(lane >= 124, tile(left, 1), tile(left, 0)), 8, 1)
    out[:, 0:128] = tile(right, 1)
    out[:, 128:256] = jnp.where((lane >= 4) & (lane < 12), edge, tile(right, 0))


def rows_kernel(left, right, cross, intra, out1, out2):
    odd = (lax.axis_index("row") % 2) == 1

    def strip(first):
        rows = pl.ds(first, 8)
        far, right_edge, left_edge = side_tiles(cross[rows, :], intra[rows, :])
        return jnp.concatenate([right_edge, far, right[rows, :], left_edge, left[rows, :]], axis=1)

    top, bottom = strip(0), strip(ROWS - 8)
    out1[...] = jnp.where(odd, top, bottom)
    out2[...] = jnp.where(odd, bottom, top)


def spread(tmp, pieces, store):
    size = pieces[0].shape[0]
    for t, piece in enumerate(pieces):
        tmp[pl.ds((size + 1) * t, size), :] = piece
    for u in range(len(pieces) // 8):
        for r in range(size):
            store(r, 8 * u, tmp[pl.ds((size + 1) * 8 * u + r, 8, stride=size + 1), :])


def block_kernel(left, right, cross, intra, out, edges, rr, lr, ob, tmp, sem):
    last = lax.axis_index("col") == lax.axis_size("col") - 1
    lane = iota((ROWS, 128), 1)
    far, right_edge, left_edge = side_tiles(cross[...], intra[...])
    r0, r1, l0, l1 = tile(right, 0), tile(right, 1), tile(left, 0), tile(left, 1)
    x = jnp.concatenate(
        [
            jnp.concatenate([jnp.where(lane < 4, r1, right_edge), far, r0], axis=1),
            jnp.concatenate([jnp.where(lane < 4, right_edge, far), r0, r1], axis=1),
        ],
        axis=0,
    )
    q, p = iota((264, 384), 0), iota((264, 384), 1)
    col = 131 - q
    rr[...] = pick_transposed(one_hot(p == jnp.where(col >= 128, col - 128, col + 256)), x)
    x = jnp.concatenate(
        [
            jnp.concatenate([jnp.where(lane < 4, l1, left_edge), l0], axis=1),
            jnp.concatenate([jnp.where(lane < 4, left_edge, l0), l1], axis=1),
        ],
        axis=0,
    )
    q, p = iota((136, 256), 0), iota((136, 256), 1)
    col = q - 4
    lr[...] = pick_transposed(one_hot(p == jnp.where(col >= 128, col - 128, col + 128)), x)
    a, b = iota((128, 128), 0), iota((128, 128), 1)
    e = a % 64
    i = jnp.where(e < 4, e, jnp.where(e < 8, e + 56, e - 4))
    band = one_hot(((a // 64) == (b // 64)) & (jnp.abs(i - b % 64) <= 4))
    band = jnp.concatenate([band, band], axis=1)
    half1 = iota((1, 128), 1) >= 64

    def cost(j):
        return jnp.abs(lr[pl.ds(j, 1), :] - rr[pl.ds(135 - j, 128), :])

    def copy(c, h):
        return pltpu.make_async_copy(ob.at[c], out.at[pl.ds(4, ROWS - 8), c, :], sem)

    total = jnp.zeros((128, 128), F32)
    for j in range(8):
        total = total + cost(j)
    steps = 128 // GROUP

    def step(s, total):
        first = s * GROUP
        outside = half1 & last & (s == steps - 1)
        top = [[], []]
        for t in range(GROUP):
            new = cost(first + t + 8)
            if t >= GROUP - 4:
                new = jnp.where(outside, 0.0, new)
            total = total + new
            done = lax.dot_general(band, halves(total), NT, preferred_element_type=F32) * SCALE
            total = total - cost(first + t)
            for h in range(2):
                c = 128 * h + first + t
                top[h].append(done[64 * h : 64 * h + 8])
                ob[c] = done[64 * h + 8 : 64 * h + 64]
                copy(c, h).start()
        for h in range(2):

            def store(r, u, value):
                edges[r, pl.ds(pl.multiple_of(128 * h + first + u, 8), 8), :] = value

            spread(tmp, top[h], store)
        return total

    lax.fori_loop(0, steps, step, total)

    pltpu.make_async_copy(ob, out.at[pl.ds(0, ROWS - 8)].reshape(COLS, ROWS - 8, 128), sem).wait()


def edge_kernel(x1, x2, partial, alias, out, rr, lr, ob, tmp, sem):
    del alias
    row = lax.axis_index("row")
    odd = (row % 2) == 1
    last = lax.axis_index("col") == lax.axis_size("col") - 1
    north = jnp.where(odd, x1[...], x2[...])
    south = jnp.where(odd, x2[...], x1[...])
    north = jnp.where(row == 0, 0.0, north)
    south = jnp.where(row == lax.axis_size("row") - 1, 0.0, south)
    both = jnp.where(iota((8, 896), 0) >= 4, north, south)
    parts = [both[:, 128 * t : 128 * t + 128] for t in range(7)]
    right = [parts[0], parts[1], parts[2], parts[3], parts[0]]
    left = [parts[4], parts[5], parts[6], parts[4]]
    lane = iota((8, 128), 1)

    def window(tiles, v, o):
        x = jnp.where(lane >= o, tiles[v], tiles[v + 1])
        return pltpu.roll(x, (128 - o) % 128, 1) if o else x

    xr, xl = [], []
    for t in range(16):
        v, o = divmod(16 * t + 120, 128)
        xr.append(jnp.concatenate([window(right, v, o), window(right, v + 1, o)], axis=1))
        v, o = divmod(16 * t + 124, 128)
        xl.append(window(left, v, o))
    q, p = iota((152, 256), 0), iota((152, 256), 1)
    rr[...] = pick_transposed(one_hot(p == 155 - q), jnp.concatenate(xr, axis=0))
    q, p = iota((24, 128), 0), iota((24, 128), 1)
    lr[...] = pick_transposed(one_hot(p == q), jnp.concatenate(xl, axis=0))
    a, b = iota((128, 128), 0), iota((128, 128), 1)
    e, r = a % 8, b % 8
    near = ((e < 4) & (r >= e + 4)) | ((e >= 4) & (r <= e - 4))
    band = one_hot(((a // 8) == (b // 8)) & near)
    band = jnp.concatenate([band, band], axis=1)
    outside = (iota((1, 128), 1) >= 120) & last

    def cost(j):
        return jnp.abs(lr[j : j + 1, :] - rr[23 - j : 151 - j, :])

    total = jnp.zeros((128, 128), F32)
    for j in range(8):
        total = total + cost(j)
    pieces = []
    for t in range(16):
        new = cost(t + 8)
        if t >= 12:
            new = jnp.where(outside, 0.0, new)
        total = total + new
        pieces.append(lax.dot_general(band, halves(total), NT, preferred_element_type=F32) * SCALE)
        total = total - cost(t)

    def store(r, u, value):
        cols = pl.ds(16 * (r // 8) + u, 8)
        ob[r % 8, cols, :] = partial[r % 8, cols, :] + value

    spread(tmp, pieces, store)
    top = pltpu.make_async_copy(ob.at[pl.ds(0, 4)], out.at[pl.ds(0, 4)], sem.at[0])
    bottom = pltpu.make_async_copy(ob.at[pl.ds(4, 4)], out.at[pl.ds(ROWS - 4, 4)], sem.at[1])
    top.start()
    bottom.start()
    top.wait()
    bottom.wait()


def params(mib):
    return pltpu.CompilerParams(vmem_limit_bytes=mib << 20)


def exchange(x, to):
    rows, cols = lax.axis_size("row"), lax.axis_size("col")
    pairs = []
    for r in range(rows):
        for c in range(cols):
            s, d = to(r, c, rows, cols)
            pairs.append((r * cols + c, s * cols + d))
    return lax.ppermute(x, ("row", "col"), pairs)


def across(r, c, rows, cols):
    d = c + 1 if c % 2 else c - 1
    return (r, d) if 0 <= d < cols else (r ^ 1, c)


def within(r, c, rows, cols):
    return r, c ^ 1


def rows_even(r, c, rows, cols):
    return r ^ 1, c


def rows_odd(r, c, rows, cols):
    return (r + 1 if r % 2 else r - 1) % rows, c


def per_device(left, right):
    shape = jax.ShapeDtypeStruct
    packed = pl.pallas_call(
        pack_kernel,
        in_specs=[VMEM, VMEM],
        out_specs=VMEM,
        out_shape=shape((ROWS, COLS), F32),
        name="pack",
    )(left, right)
    cross = exchange(packed, across)
    intra = exchange(packed, within)
    send1, send2 = pl.pallas_call(
        rows_kernel,
        in_specs=[VMEM] * 4,
        out_specs=[VMEM] * 2,
        out_shape=[shape((8, 896), F32)] * 2,
        name="pack_rows",
    )(left, right, cross, intra)
    got1 = exchange(send1, rows_even)
    got2 = exchange(send2, rows_odd)
    out, edges = pl.pallas_call(
        block_kernel,
        in_specs=[VMEM] * 4,
        out_specs=[HBM, VMEM],
        out_shape=[shape((ROWS, COLS, ND), F32), shape((8, COLS, ND), F32)],
        scratch_shapes=[
            pltpu.VMEM((264, 128), F32),
            pltpu.VMEM((136, 128), F32),
            pltpu.VMEM((COLS, ROWS - 8, 128), F32),
            pltpu.VMEM((GROUP * 9 + 8, 128), F32),
            pltpu.SemaphoreType.DMA,
        ],
        compiler_params=params(24),
        cost_estimate=pl.CostEstimate(flops=2 * 128 * 128 * 256 * 128, bytes_accessed=9 << 20, transcendentals=0),
        name="block",
    )(left, right, cross, intra)
    return pl.pallas_call(
        edge_kernel,
        in_specs=[VMEM, VMEM, VMEM, HBM],
        out_specs=HBM,
        out_shape=shape((ROWS, COLS, ND), F32),
        scratch_shapes=[
            pltpu.VMEM((152, 128), F32),
            pltpu.VMEM((24, 128), F32),
            pltpu.VMEM((8, COLS, 128), F32),
            pltpu.VMEM((16 * 129 + 8, 128), F32),
            pltpu.SemaphoreType.DMA((2,)),
        ],
        input_output_aliases={3: 0},
        compiler_params=params(16),
        name="edge",
    )(got1, got2, edges, out)


def solution(mesh):
    specs = (P("row", "col"), P("row", "col"))
    return jax.shard_map(
        per_device, mesh=mesh, in_specs=specs, out_specs=P("row", "col", None), check_vma=False
    )
```

time: 175 us -> 26.8 us (0.15)
  the two profiles are of different devices: /device:TPU:27 before, /device:TPU:24 now
where the time goes in v1:
time: 26.8 us; the launch traced here: 26.5 us
  Pallas kernels  10.5 us (39%)
  starting transfers between devices  9.74 us (36%)
  local copies, waits for them, and re-layouts  3.99 us (15%)
  waiting for transfers between devices  2.22 us (8%)
    ppermute x4, starting transfers between devices, exchange(): return lax.ppermute(x, ('row', 'col'), pairs)  9.74 us
    pallas_call x1, Pallas kernels, per_device(): pl.pallas_call(block_kernel, in_specs=[VMEM] * 4, out_specs=[HBM, VMEM],...  5.27 us
    unnamed x12, local copies, waits for them, and re-layouts  3.99 us
    ppermute x4, waiting for transfers between devices, exchange(): return lax.ppermute(x, ('row', 'col'), pairs)  2.22 us
    pallas_call x1, Pallas kernels, per_device(): pl.pallas_call(edge_kernel, in_specs=[VMEM, VMEM, VMEM, HBM], out_specs=H...  2 us
    pallas_call x1, Pallas kernels, per_device(): pl.pallas_call(rows_kernel, in_specs=[VMEM] * 4, out_specs=[VMEM] * 2, ou...  1.63 us
    pallas_call x1, Pallas kernels, per_device(): pl.pallas_call(pack_kernel, in_specs=[VMEM, VMEM], out_specs=VMEM, out_sh...  1.58 us
  transfers between devices with their start and end apart: 4, of which 1 were waited for; matrix products, arithmetic and copies ran while one was open for 0% of the time, Pallas kernels for 20%

profile of v1, /device:TPU:24, one launch (start us, length us, event | category | flops | bytes accessed | tf_op | source)
XLA Modules:
  0.0 26.5 jit_solution(17748331133089995530)
XLA Ops:
  0.0 1.6 %pack.1 = f32[64,256]{1,0:T(8,128)} custom-call(f32[64,256]{1,0:T(8,128)} %left.5, f32[64,256]{1,0:T(8,128)} %right.5), custom_call_target="tpu_custom_call" | custom-call | tf_op jit(solution)/shard_map/pack/pallas_call | solution.py:261
  1.6 0.0 collective-permute-start.1
  1.6 6.1 %collective-permute-start = (f32[64,256]{1,0:T(8,128)}, f32[64,256]{1,0:T(8,128)S(1)}, u32[]{:S(2)}, u32[]{:S(2)}) collective-permute-start(f32[64,256]{1,0:T(8,128)} %pack.1), channel_id=1, source_target_pairs={{0,64},{1,2},{2,1},{3,4},{4,3},{5,6},{6,5},{7,8},{8,7},{9,10},{10,... | collective-permute-start | bytes 196616 | tf_op jit(solution)/shard_map/ppermute | solution.py:239
  7.7 0.0 collective-permute-done.1.intra
  7.7 0.0 copy-start.2
  7.7 2.2 %collective-permute-done.cross = f32[64,256]{1,0:T(8,128)S(1)} collective-permute-done((f32[64,256]{1,0:T(8,128)}, f32[64,256]{1,0:T(8,128)S(1)}, u32[]{:S(2)}, u32[]{:S(2)}) %collective-permute-start) | collective-permute-done | bytes 65568 | tf_op jit(solution)/shard_map/ppermute | solution.py:239
  10.0 0.0 copy-done.2
  10.0 0.0 copy-start.4
  10.0 0.6 %copy-done.4 = f32[64,256]{1,0:T(8,128)} copy-done((f32[64,256]{1,0:T(8,128)}, f32[64,256]{1,0:T(8,128)S(1)}, u32[]{:S(2)}) %copy-start.4) | copy-done | bytes 65560
  10.6 1.6 %pack_rows.1 = (f32[8,896]{1,0:T(8,128)}, f32[8,896]{1,0:T(8,128)}) custom-call(f32[64,256]{1,0:T(8,128)} %left.5, f32[64,256]{1,0:T(8,128)} %right.5, f32[64,256]{1,0:T(8,128)} %copy-done.4, f32[64,256]{1,0:T(8,128)} %copy-done.2), custom_call_target="tpu_custom_call" | custom-call | tf_op jit(solution)/shard_map/pack_rows/pallas_call | solution.py:270
  12.2 1.5 %collective-permute-start.2 = (f32[8,896]{1,0:T(8,128)}, f32[8,896]{1,0:T(8,128)S(1)}, u32[]{:S(2)}, u32[]{:S(2)}) collective-permute-start(f32[8,896]{1,0:T(8,128)} %get-tuple-element.9), channel_id=1, source_target_pairs={{0,64},{1,65},{2,66},{3,67},{4,68},{5,69},{6,70},{7,71},{8,72},{9,... | collective-permute-start | bytes 86024 | tf_op jit(solution)/shard_map/ppermute | solution.py:239
  13.7 2.1 %collective-permute-start.3 = (f32[8,896]{1,0:T(8,128)}, f32[8,896]{1,0:T(8,128)S(1)}, u32[]{:S(2)}, u32[]{:S(2)}) collective-permute-start(f32[8,896]{1,0:T(8,128)} %get-tuple-element.10), channel_id=1, source_target_pairs={{0,192},{1,193},{2,194},{3,195},{4,196},{5,197},{6,198},{7,199},{8... | collective-permute-start | bytes 86024 | tf_op jit(solution)/shard_map/ppermute | solution.py:239
  15.8 0.0 copy-start
  15.8 0.8 %copy-done = f32[64,256]{1,0:T(8,128)S(1)} copy-done((f32[64,256]{1,0:T(8,128)S(1)}, f32[64,256]{1,0:T(8,128)}, u32[]{:S(2)}) %copy-start) | copy-done | bytes 65560
  16.6 0.0 copy-start.1
  16.6 0.8 %copy-done.1 = f32[64,256]{1,0:T(8,128)S(1)} copy-done((f32[64,256]{1,0:T(8,128)S(1)}, f32[64,256]{1,0:T(8,128)}, u32[]{:S(2)}) %copy-start.1) | copy-done | bytes 65560
  17.5 0.0 copy-start.3
  17.5 0.8 %copy-done.3 = f32[64,256]{1,0:T(8,128)S(1)} copy-done((f32[64,256]{1,0:T(8,128)S(1)}, f32[64,256]{1,0:T(8,128)}, u32[]{:S(2)}) %copy-start.3) | copy-done | bytes 65560
  18.3 0.0 copy-start.5
  18.3 0.8 %copy-done.5 = f32[64,256]{1,0:T(8,128)S(1)} copy-done((f32[64,256]{1,0:T(8,128)S(1)}, f32[64,256]{1,0:T(8,128)}, u32[]{:S(2)}) %copy-start.5) | copy-done | bytes 65560
  19.2 5.3 %block.1 = (f32[64,256,128]{2,1,0:T(8,128)}, f32[8,256,128]{2,1,0:T(8,128)S(1)}) custom-call(f32[64,256]{1,0:T(8,128)S(1)} %copy-done, f32[64,256]{1,0:T(8,128)S(1)} %copy-done.1, f32[64,256]{1,0:T(8,128)S(1)} %copy-done.5, f32[64,256]{1,0:T(8,128)S(1)} %copy-done.3), custom_call_target="tpu_custom_call" | custom-call | flops 1073741824 | bytes 9437184 | tf_op jit(solution)/shard_map/block/pallas_call | solution.py:279
  24.4 0.0 collective-permute-done.2.x1
  24.5 0.0 collective-permute-done.3.x2
  24.5 2.0 %edge.1 = f32[64,256,128]{2,1,0:T(8,128)} custom-call(f32[8,896]{1,0:T(8,128)S(1)} %collective-permute-done.2.x1, f32[8,896]{1,0:T(8,128)S(1)} %collective-permute-done.3.x2, f32[8,256,128]{2,1,0:T(8,128)S(1)} %get-tuple-element.11.partial, f32[64,256,128]{2,1,0:T(8,128)} %get-tuple-element.12.alias), custom_call_target="tpu_custom_call", output_to_operand_aliasing={{}: (3, {})} | custom-call | tf_op jit(solution)/shard_map/edge/pallas_call | solution.py:295
Async XLA Ops:
  1.6 6.2 %collective-permute-start.1 = (f32[64,256]{1,0:T(8,128)}, f32[64,256]{1,0:T(8,128)S(1)}, u32[]{:S(2)}, u32[]{:S(2)}) collective-permute-start(f32[64,256]{1,0:T(8,128)} %pack.1), channel_id=1, source_target_pairs={{0,1},{1,0},{2,3},{3,2},{4,5},{5,4},{6,7},{7,6},{8,9},{9,8},{10,11... | collective-permute-start | bytes 196616 | tf_op jit(solution)/shard_map/ppermute | solution.py:239
  1.6 8.4 %collective-permute-start = (f32[64,256]{1,0:T(8,128)}, f32[64,256]{1,0:T(8,128)S(1)}, u32[]{:S(2)}, u32[]{:S(2)}) collective-permute-start(f32[64,256]{1,0:T(8,128)} %pack.1), channel_id=1, source_target_pairs={{0,64},{1,2},{2,1},{3,4},{4,3},{5,6},{6,5},{7,8},{8,7},{9,10},{10,... | collective-permute-start | bytes 196616 | tf_op jit(solution)/shard_map/ppermute | solution.py:239
  7.7 2.2 %copy-start.2 = (f32[64,256]{1,0:T(8,128)}, f32[64,256]{1,0:T(8,128)S(1)}, u32[]{:S(2)}) copy-start(f32[64,256]{1,0:T(8,128)S(1)} %collective-permute-done.1.intra) | copy-start | bytes 196612
  10.0 0.6 %copy-start.4 = (f32[64,256]{1,0:T(8,128)}, f32[64,256]{1,0:T(8,128)S(1)}, u32[]{:S(2)}) copy-start(f32[64,256]{1,0:T(8,128)S(1)} %collective-permute-done.cross) | copy-start | bytes 196612
  12.2 12.2 %collective-permute-start.2 = (f32[8,896]{1,0:T(8,128)}, f32[8,896]{1,0:T(8,128)S(1)}, u32[]{:S(2)}, u32[]{:S(2)}) collective-permute-start(f32[8,896]{1,0:T(8,128)} %get-tuple-element.9), channel_id=1, source_target_pairs={{0,64},{1,65},{2,66},{3,67},{4,68},{5,69},{6,70},{7,71},{8,72},{9,... | collective-permute-start | bytes 86024 | tf_op jit(solution)/shard_map/ppermute | solution.py:239
  13.7 10.7 %collective-permute-start.3 = (f32[8,896]{1,0:T(8,128)}, f32[8,896]{1,0:T(8,128)S(1)}, u32[]{:S(2)}, u32[]{:S(2)}) collective-permute-start(f32[8,896]{1,0:T(8,128)} %get-tuple-element.10), channel_id=1, source_target_pairs={{0,192},{1,193},{2,194},{3,195},{4,196},{5,197},{6,198},{7,199},{8... | collective-permute-start | bytes 86024 | tf_op jit(solution)/shard_map/ppermute | solution.py:239
  15.8 0.8 %copy-start = (f32[64,256]{1,0:T(8,128)S(1)}, f32[64,256]{1,0:T(8,128)}, u32[]{:S(2)}) copy-start(f32[64,256]{1,0:T(8,128)} %left.5) | copy-start | bytes 196612
  16.6 0.8 %copy-start.1 = (f32[64,256]{1,0:T(8,128)S(1)}, f32[64,256]{1,0:T(8,128)}, u32[]{:S(2)}) copy-start(f32[64,256]{1,0:T(8,128)} %right.5) | copy-start | bytes 196612
  17.5 0.8 %copy-start.3 = (f32[64,256]{1,0:T(8,128)S(1)}, f32[64,256]{1,0:T(8,128)}, u32[]{:S(2)}) copy-start(f32[64,256]{1,0:T(8,128)} %copy-done.2) | copy-start | bytes 196612
  18.3 0.8 %copy-start.5 = (f32[64,256]{1,0:T(8,128)S(1)}, f32[64,256]{1,0:T(8,128)}, u32[]{:S(2)}) copy-start(f32[64,256]{1,0:T(8,128)} %copy-done.4) | copy-start | bytes 196612

commit v2 on v0

v2 whole, which is shorter than its diff:
```python
import functools

import jax
import jax.numpy as jnp
from jax import lax
from jax.experimental import pallas as pl
from jax.experimental.pallas import tpu as pltpu
from jax.sharding import PartitionSpec as P

ND = 128
ROWS = 64
COLS = 256
F32 = jnp.float32
BF16 = jnp.bfloat16
NT = (((1,), (1,)), ((), ()))
SCALE = 1.0 / 81.0
LATE = 16
VMEM = pl.BlockSpec(memory_space=pltpu.VMEM)
HBM = pl.BlockSpec(memory_space=pl.ANY)


def iota(shape, dim):
    return lax.broadcasted_iota(jnp.int32, shape, dim)


def tile(ref, t):
    return ref[:, 128 * t : 128 * t + 128]


def one_hot(mask):
    return jnp.where(mask, 1.0, 0.0).astype(BF16)


def halves(x):
    high = x.astype(BF16)
    low = (x - high.astype(F32)).astype(BF16)
    return jnp.concatenate([high, low], axis=1)


def pick_transposed(chosen, x):
    a = x.astype(BF16)
    rest = x - a.astype(F32)
    b = rest.astype(BF16)
    c = (rest - b.astype(F32)).astype(BF16)
    dot = functools.partial(lax.dot_general, dimension_numbers=NT, preferred_element_type=F32)
    return (dot(chosen, c) + dot(chosen, b)) + dot(chosen, a)


def neighbours(cross, intra):
    c = lax.axis_index("col")
    odd = (c % 2) == 1
    west = jnp.where(odd, intra, cross)
    east = jnp.where(odd, cross, intra)
    west = jnp.where(c == 0, 0.0, west)
    east = jnp.where(c == lax.axis_size("col") - 1, 0.0, east)
    return west, east


def turn(x, left):
    left %= 128
    return pltpu.roll(x, 128 - left, 1) if left else x


def side_tiles(west, east, groups):
    far = jnp.concatenate([west[8 * g : 8 * g + 8] for g in groups], axis=0)
    west, east = west[ROWS:], east[ROWS:]
    lane = iota((8, 128), 1)
    both = jnp.where(lane % 16 >= 8, east, west)
    right = [jnp.where(lane < 4, turn(east, 16 * g), turn(west, 16 * g + 16)) for g in groups]
    left = [turn(both, 16 * g + 8) for g in groups]
    return far, jnp.concatenate(right, axis=0), jnp.concatenate(left, axis=0)


def pack_kernel(both, out, images):
    images[...] = both[...]
    lane = iota((8, 128), 1)
    edges = jnp.zeros((8, 128), F32)
    for g in range(ROWS // 8):
        l0, l1, r0, r1 = [images[8 * g : 8 * g + 8, 128 * t : 128 * t + 128] for t in range(4)]
        out[8 * g : 8 * g + 8, :] = r1
        left = turn(jnp.where(lane >= 124, l1, l0), -8)
        some = jnp.where(lane < 4, r0, jnp.where(lane < 12, left, turn(r0, -16)))
        edges = jnp.where(lane // 16 == g, turn(some, -16 * g), edges)
    out[ROWS:, :] = edges


def copy_kernel(x, out):
    out[...] = x[...]


def rows_kernel(images, cross, intra, out1, out2):
    odd = (lax.axis_index("row") % 2) == 1
    west, east = neighbours(cross[...], intra[...])

    def strip(g):
        far, right_edge, left_edge = side_tiles(west, east, [g])
        rows = images[8 * g : 8 * g + 8, :]
        return jnp.concatenate([right_edge, far, rows[:, 256:512], left_edge, rows[:, 0:256]], axis=1)

    top, bottom = strip(0), strip(ROWS // 8 - 1)
    out1[...] = jnp.where(odd, top, bottom)
    out2[...] = jnp.where(odd, bottom, top)


def window(tiles, start):
    v, o = divmod(start, 128)
    if o == 0:
        return tiles[v]
    lane = iota(tiles[v].shape, 1)
    return pltpu.roll(jnp.where(lane >= o, tiles[v], tiles[v + 1]), 128 - o, 1)


def lay_out(right, left, bases, n, rr, lr):
    x = [jnp.concatenate([window(right, b + 120), window(right, b + 248)], axis=1) for b in bases]
    size = -(-(n + 135) // 8) * 8
    q, p = iota((size, 256), 0), iota((size, 256), 1)
    rr[pl.ds(0, size), :] = pick_transposed(one_hot(p == n + 139 - q), jnp.concatenate(x, axis=0))
    x = [window(left, b + 124) for b in bases]
    size = -(-(n + 8) // 8) * 8
    q, p = iota((size, 128), 0), iota((size, 128), 1)
    lr[pl.ds(0, size), :] = pick_transposed(one_hot(p == q), jnp.concatenate(x, axis=0))


def own_band():
    a, b = iota((128, 128), 0), iota((128, 128), 1)
    e = a % 64
    i = jnp.where(e < 4, e, jnp.where(e < 8, e + 56, e - 4))
    band = one_hot(((a // 64) == (b // 64)) & (jnp.abs(i - b % 64) <= 4))
    return jnp.concatenate([band, band], axis=1)


def sweep(rr, lr, ring, band, bases, n, emit, outside=None):
    def cost(j):
        new = jnp.abs(lr[j : j + 1, :] - rr[n + 7 - j : n + 135 - j, :])
        if outside is not None:
            new = outside(j, new)
        if j < n - 1:
            ring[j % 16] = new
        return new

    total = cost(0)
    for j in range(1, 8):
        total = total + cost(j)
    for k in range(n):
        total = total + cost(k + 8)
        emit(k, lax.dot_general(band, halves(total), NT, preferred_element_type=F32) * SCALE)
        if k < n - 1:
            total = total - ring[k % 16]


def columns(segments):
    return [b + k for bases, n, ks in segments for k in ks for b in bases]


INNER = ((132, 192), 60)
OUTER = ((0, 66), 66)
EAST = ((252, 254), 2)
FIRST = [*columns([(*EAST, range(2)), (*OUTER, range(OUTER[1] - LATE))])]
SECOND = columns([(*OUTER, range(OUTER[1] - LATE, OUTER[1]))])
BEFORE = columns([(*INNER, range(INNER[1]))])


def ship(blocks, out, cols, sem):
    for o, c in enumerate(cols):
        pltpu.make_async_copy(blocks.at[o], out.at[pl.ds(4, ROWS - 8), c, :], sem).start()
    return pltpu.make_async_copy(blocks, blocks, sem)


def inner_kernel(images, ready, edges, rr, lr, ring):
    l0, l1, r0, r1 = [tile(images, t) for t in range(4)]
    bases, n = INNER
    lay_out([r0, r0, r0, r1, r1], [l0, l0, l1, l1], bases, n, rr, lr)

    def emit(k, done):
        for h in range(2):
            edges[bases[h] + k] = done[64 * h : 64 * h + 8]
            ready[2 * k + h] = done[64 * h + 8 : 64 * h + 64]

    sweep(rr, lr, ring, own_band(), bases, n, emit)


def outer_kernel(images, cross, intra, ready, part, out, late, edges, rr, lr, rr2, lr2, ring, ob, sem):
    del part
    shipped = ship(ready, out, BEFORE, sem.at[0])
    last = lax.axis_index("col") == lax.axis_size("col") - 1
    far, right_edge, left_edge = side_tiles(*neighbours(cross[...], intra[...]), range(ROWS // 8))
    l0, l1, r0, r1 = [tile(images, t) for t in range(4)]
    rights = [right_edge, far, r0, r1, right_edge]
    lefts = [left_edge, l0, l1, left_edge]
    band = own_band()
    lay_out(rights, lefts, *OUTER, rr, lr)
    lay_out(rights, lefts, *EAST, rr2, lr2)
    lane = iota((1, 128), 1)

    def emit(bases, k, done):
        for h in range(2):
            c = bases[h] + k
            edges[c] = done[64 * h : 64 * h + 8]
            block = done[64 * h + 8 : 64 * h + 64]
            if c in SECOND:
                late[SECOND.index(c)] = block
            else:
                o = FIRST.index(c)
                ob[o] = block
                pltpu.make_async_copy(ob.at[o], out.at[pl.ds(4, ROWS - 8), c, :], sem.at[1]).start()

    def outside(j, new):
        if j < 6:
            return new
        return jnp.where(last & (lane >= 0 if j >= 8 else lane >= 64), 0.0, new)

    sweep(rr2, lr2, ring, band, *EAST, functools.partial(emit, EAST[0]), outside)
    sweep(rr, lr, ring, band, *OUTER, functools.partial(emit, OUTER[0]))
    shipped.wait()
    pltpu.make_async_copy(ob, ob, sem.at[1]).wait()


def spread(tmp, pieces, store):
    size = pieces[0].shape[0]
    for t, piece in enumerate(pieces):
        tmp[pl.ds((size + 1) * t, size), :] = piece
    for u in range(len(pieces) // 8):
        for r in range(size):
            store(r, 8 * u, tmp[pl.ds((size + 1) * 8 * u + r, 8, stride=size + 1), :])


def edge_kernel(x1, x2, partial, late, alias, out, rr, lr, ring, ob, tmp, sem):
    del alias
    shipped = ship(late, out, SECOND, sem.at[0])
    row = lax.axis_index("row")
    odd = (row % 2) == 1
    last = lax.axis_index("col") == lax.axis_size("col") - 1
    north = jnp.where(odd, x1[...], x2[...])
    south = jnp.where(odd, x2[...], x1[...])
    north = jnp.where(row == 0, 0.0, north)
    south = jnp.where(row == lax.axis_size("row") - 1, 0.0, south)
    both = jnp.where(iota((8, 896), 0) >= 4, north, south)
    parts = [both[:, 128 * t : 128 * t + 128] for t in range(7)]
    right = [parts[0], parts[1], parts[2], parts[3], parts[0]]
    left = [parts[4], parts[5], parts[6], parts[4]]
    bases = [16 * t for t in range(16)]
    lay_out(right, left, bases, 16, rr, lr)
    a, b = iota((128, 128), 0), iota((128, 128), 1)
    e, r = a % 8, b % 8
    near = ((e < 4) & (r >= e + 4)) | ((e >= 4) & (r <= e - 4))
    band = one_hot(((a // 8) == (b // 8)) & near)
    band = jnp.concatenate([band, band], axis=1)
    lane = iota((1, 128), 1)
    pieces = []

    def outside(j, new):
        return jnp.where((lane >= 120) & last, 0.0, new) if j >= 20 else new

    def copies(half):
        cols = pl.ds(8 * half, 8)
        source, target = ob.reshape(8, 16, 16, ND), out.reshape(ROWS, 16, 16, ND)
        return [
            pltpu.make_async_copy(source.at[pl.ds(0, 4), :, cols], target.at[pl.ds(0, 4), :, cols], sem.at[1 + half]),
            pltpu.make_async_copy(source.at[pl.ds(4, 4), :, cols], target.at[pl.ds(ROWS - 4, 4), :, cols], sem.at[3 + half]),
        ]

    def emit(k, done):
        pieces.append(done + jnp.concatenate([partial[b + k] for b in bases], axis=0))
        if k % 8 < 7:
            return

        def store(r, u, value):
            ob[r % 8, pl.ds(16 * (r // 8) + k - 7, 8), :] = value

        spread(tmp.at[k // 8], pieces, store)
        pieces.clear()
        for copy in copies(k // 8):
            copy.start()

    sweep(rr, lr, ring, band, bases, 16, emit, outside)
    for copy in [shipped, *copies(0), *copies(1)]:
        copy.wait()


def params(mib):
    return pltpu.CompilerParams(vmem_limit_bytes=mib << 20)


def exchange(x, to):
    rows, cols = lax.axis_size("row"), lax.axis_size("col")
    pairs = []
    for r in range(rows):
        for c in range(cols):
            s, d = to(r, c, rows, cols)
            pairs.append((r * cols + c, s * cols + d))
    return lax.ppermute(x, ("row", "col"), pairs)


def across(r, c, rows, cols):
    d = c + 1 if c % 2 else c - 1
    return (r, d) if 0 <= d < cols else (r ^ 1, c)


def within(r, c, rows, cols):
    return r, c ^ 1


def rows_even(r, c, rows, cols):
    return r ^ 1, c


def rows_odd(r, c, rows, cols):
    s = r + 1 if r % 2 else r - 1
    return (s, c) if 0 <= s < rows else (r, c ^ 1)


def per_device(left, right):
    shape = jax.ShapeDtypeStruct
    packed, images = pl.pallas_call(
        pack_kernel,
        in_specs=[VMEM],
        out_specs=[VMEM] * 2,
        out_shape=[shape((ROWS + 8, 128), F32), shape((ROWS, 2 * COLS), F32)],
        compiler_params=params(1),
        name="pack",
    )(jnp.concatenate([left, right], axis=1))
    cross = exchange(packed, across)
    intra = exchange(pl.pallas_call(copy_kernel, in_specs=[VMEM], out_specs=VMEM, out_shape=shape((ROWS + 8, 128), F32), compiler_params=params(1), name="again")(packed), within)
    volume = shape((ROWS, COLS, ND), F32)
    sides = shape((COLS, 8, ND), F32)

    def blocks(cols):
        return shape((len(cols), ROWS - 8, ND), F32)

    def scratch(*counts):
        sizes = [size for n in counts for size in (n + 135, n + 8)]
        return [pltpu.VMEM((-(-size // 8) * 8, 128), F32) for size in sizes] + [pltpu.VMEM((16, 128, 128), F32)]

    def cost(cols):
        return pl.CostEstimate(
            flops=2 * 128 * 128 * 128 * len(cols), bytes_accessed=len(cols) << 15, transcendentals=0
        )

    ready, edges = pl.pallas_call(
        inner_kernel,
        in_specs=[VMEM],
        out_specs=[VMEM] * 2,
        out_shape=[blocks(BEFORE), sides],
        scratch_shapes=scratch(INNER[1]),
        compiler_params=params(4),
        cost_estimate=cost(BEFORE),
        name="inner",
    )(images)
    send1, send2 = pl.pallas_call(
        rows_kernel,
        in_specs=[VMEM] * 3,
        out_specs=[VMEM] * 2,
        out_shape=[shape((8, 896), F32)] * 2,
        compiler_params=params(1),
        name="pack_rows",
    )(images, cross, intra)
    got1 = exchange(send1, rows_even)
    got2 = exchange(send2, rows_odd)
    out, late, edges = pl.pallas_call(
        outer_kernel,
        in_specs=[VMEM] * 5,
        out_specs=[HBM, VMEM, VMEM],
        out_shape=[volume, blocks(SECOND), sides],
        scratch_shapes=scratch(OUTER[1], EAST[1])
        + [pltpu.VMEM(blocks(FIRST).shape, F32), pltpu.SemaphoreType.DMA((2,))],
        input_output_aliases={4: 2},
        compiler_params=params(8),
        cost_estimate=cost(FIRST + SECOND),
        name="outer",
    )(images, cross, intra, ready, edges)
    return pl.pallas_call(
        edge_kernel,
        in_specs=[VMEM, VMEM, VMEM, VMEM, HBM],
        out_specs=HBM,
        out_shape=volume,
        scratch_shapes=scratch(16)
        + [
            pltpu.VMEM((8, COLS, ND), F32),
            pltpu.VMEM((2, 8 * 129, 128), F32),
            pltpu.SemaphoreType.DMA((5,)),
        ],
        input_output_aliases={4: 0},
        compiler_params=params(6),
        name="edge",
    )(got1, got2, edges, late, out)


def solution(mesh):
    specs = (P("row", "col"), P("row", "col"))
    return jax.shard_map(
        per_device, mesh=mesh, in_specs=specs, out_specs=P("row", "col", None), check_vma=False
    )
```

time: 175 us -> 16.2 us (0.09); the launches traced: 173 us -> 16.1 us
  other arithmetic: 96.3 us -> 0.88 us
  local copies, waits for them, and re-layouts: 46.7 us -> 0 us
  starting transfers between devices: 20.6 us -> 8.34 us
  waiting for transfers between devices: 9.12 us -> 0.01 us
  Pallas kernels: 0 us -> 6.8 us
    div x1 -> x0, other arithmetic: 59.9 us -> none  [per_device(): return total / 81.0]
    add x1 -> x0, other arithmetic: 34.5 us -> none  [window_rows(): summed = summed + padded[offset:offset + count]]
    unnamed x134 -> x0, local copies, waits for them, and re-layouts: 15.1 us -> none
    slice x4 -> x0, local copies, waits for them, and re-layouts: 12.4 us -> none  [the longest x3 8.62 us: extended(): last = lax.slice_in_dim(value, length - width, length, axis=dim)]
    ppermute x5 -> x4, starting transfers between devices: 20.6 us -> 8.34 us  [exchange(): return lax.ppermute(x, ('row', 'col'), pairs)]
    div x1 -> x0, local copies, waits for them, and re-layouts: 9.26 us -> none  [per_device(): return total / 81.0]
    ppermute x5 -> x4, waiting for transfers between devices: 9.12 us -> 0.01 us  [exchange(): return lax.ppermute(x, ('row', 'col'), pairs)]
    ppermute x2 -> x0, local copies, waits for them, and re-layouts: 8.95 us -> none  [the longest x1 4.49 us: extended(): after = lax.ppermute(first, axis, down)]
  transfers between devices with their start and end apart: 5 -> 4, of which waited for: 3 -> 0; matrix products, arithmetic and copies ran while one was open for 5% -> 0% of each run, Pallas kernels for 0% -> 29%
where the time goes in v2:
time: 16.2 us; the launch traced here: 16.1 us
  starting transfers between devices  8.34 us (51%)
  Pallas kernels  6.8 us (42%)
  other arithmetic  0.88 us (5%)
    ppermute x4, starting transfers between devices, exchange(): return lax.ppermute(x, ('row', 'col'), pairs)  8.34 us
    pallas_call x1, Pallas kernels, per_device(): pl.pallas_call(outer_kernel, in_specs=[VMEM] * 5, out_specs=[HBM, VMEM, V...  2.8 us
    pallas_call x1, Pallas kernels, per_device(): pl.pallas_call(inner_kernel, in_specs=[VMEM], out_specs=[VMEM] * 2, out_s...  1.91 us
    pallas_call x1, Pallas kernels, per_device(): pl.pallas_call(edge_kernel, in_specs=[VMEM, VMEM, VMEM, VMEM, HBM], out_s...  1.84 us
    concatenate x1, other arithmetic, per_device(): jnp.concatenate([left, right], axis=1)  0.88 us
  transfers between devices with their start and end apart: 4, of which 0 were waited for; matrix products, arithmetic and copies ran while one was open for 0% of the time, Pallas kernels for 29%

profile of v2, /device:TPU:27, one launch (start us, length us, event | category | flops | bytes accessed | tf_op | source)
XLA Modules:
  0.0 16.1 jit_solution(8785828345336218701)
XLA Ops:
  0.0 0.9 %pad_maximum_fusion.both = f32[64,512]{1,0:T(8,128)S(1)} fusion(f32[64,256]{1,0:T(8,128)} %param.3, f32[64,256]{1,0:T(8,128)} %param.2), kind=kLoop, calls=%fused_computation | loop fusion | flops 32768 | bytes 262144 | tf_op jit(solution)/shard_map/concatenate | solution.py:321
  0.9 0.1 pack.1
  1.0 2.2 %collective-permute-start = (f32[72,128]{1,0:T(8,128)S(1)}, f32[72,128]{1,0:T(8,128)S(1)}, u32[]{:S(2)}, u32[]{:S(2)}) collective-permute-start(f32[72,128]{1,0:T(8,128)S(1)} %get-tuple-element.15.x), channel_id=1, source_target_pairs={{0,64},{1,2},{2,1},{3,4},{4,3},{5,6},{6,5},{7,8},{8,7},{9,10},{10,... | collective-permute-start | bytes 110600 | tf_op jit(solution)/shard_map/ppermute | solution.py:291
  3.3 4.0 %collective-permute-start.1 = (f32[72,128]{1,0:T(8,128)S(1)}, f32[72,128]{1,0:T(8,128)S(1)}, u32[]{:S(2)}, u32[]{:S(2)}) collective-permute-start(f32[72,128]{1,0:T(8,128)S(1)} %again.1), channel_id=1, source_target_pairs={{0,1},{1,0},{2,3},{3,2},{4,5},{5,4},{6,7},{7,6},{8,9},{9,8},{10,11... | collective-permute-start | bytes 110600 | tf_op jit(solution)/shard_map/ppermute | solution.py:291
  7.2 1.9 %inner.1 = (f32[120,56,128]{2,1,0:T(8,128)S(1)}, f32[256,8,128]{2,1,0:T(8,128)S(1)}) custom-call(f32[64,512]{1,0:T(8,128)S(1)} %get-tuple-element.14.images), custom_call_target="tpu_custom_call" | custom-call | flops 503316480 | bytes 3932160 | tf_op jit(solution)/shard_map/inner/pallas_call | solution.py:339
  9.1 0.0 collective-permute-done.1.intra
  9.2 0.0 collective-permute-done.cross
  9.2 0.1 pack_rows.1
  9.3 0.3 %collective-permute-start.2 = (f32[8,896]{1,0:T(8,128)S(1)}, f32[8,896]{1,0:T(8,128)S(1)}, u32[]{:S(2)}, u32[]{:S(2)}) collective-permute-start(f32[8,896]{1,0:T(8,128)S(1)} %get-tuple-element.16), channel_id=1, source_target_pairs={{0,64},{1,65},{2,66},{3,67},{4,68},{5,69},{6,70},{7,71},{8,72},{9,... | collective-permute-start | bytes 86024 | tf_op jit(solution)/shard_map/ppermute | solution.py:291
  9.5 1.9 %collective-permute-start.3 = (f32[8,896]{1,0:T(8,128)S(1)}, f32[8,896]{1,0:T(8,128)S(1)}, u32[]{:S(2)}, u32[]{:S(2)}) collective-permute-start(f32[8,896]{1,0:T(8,128)S(1)} %get-tuple-element.17), channel_id=1, source_target_pairs={{0,1},{1,0},{2,3},{3,2},{4,5},{5,4},{6,7},{7,6},{8,9},{9,8},{10,11... | collective-permute-start | bytes 86024 | tf_op jit(solution)/shard_map/ppermute | solution.py:291
  11.4 2.8 %outer.1 = (f32[64,256,128]{2,1,0:T(8,128)}, f32[32,56,128]{2,1,0:T(8,128)S(1)}, f32[256,8,128]{2,1,0:T(8,128)S(1)}) custom-call(f32[64,512]{1,0:T(8,128)S(1)} %get-tuple-element.14.images, f32[72,128]{1,0:T(8,128)S(1)} %collective-permute-done.cross, f32[72,128]{1,0:T(8,128)S(1)} %collective-permute-done.1.intra, ...), custom_call_target="tpu_custom_call", output_to_operand_aliasing={{2}: (4, {})} | custom-call | flops 570425344 | bytes 4456448 | tf_op jit(solution)/shard_map/outer/pallas_call | solution.py:359
  14.2 0.0 collective-permute-done.2.x1
  14.2 0.0 collective-permute-done.3.x2
  14.2 1.8 %edge.1 = f32[64,256,128]{2,1,0:T(8,128)} custom-call(f32[8,896]{1,0:T(8,128)S(1)} %collective-permute-done.2.x1, f32[8,896]{1,0:T(8,128)S(1)} %collective-permute-done.3.x2, f32[256,8,128]{2,1,0:T(8,128)S(1)} %get-tuple-element.20.partial, f32[32,56,128]{2,1,0:T(8,128)S(1)} %get-tuple-element.21.late, ...), custom_call_target="tpu_custom_call", output_to_operand_aliasing={{}: (4, {})} | custom-call | tf_op jit(solution)/shard_map/edge/pallas_call | solution.py:371
  (1 shorter events, 0.0 us)
Async XLA Ops:
  1.0 8.1 %collective-permute-start = (f32[72,128]{1,0:T(8,128)S(1)}, f32[72,128]{1,0:T(8,128)S(1)}, u32[]{:S(2)}, u32[]{:S(2)}) collective-permute-start(f32[72,128]{1,0:T(8,128)S(1)} %get-tuple-element.15.x), channel_id=1, source_target_pairs={{0,64},{1,2},{2,1},{3,4},{4,3},{5,6},{6,5},{7,8},{8,7},{9,10},{10,... | collective-permute-start | bytes 110600 | tf_op jit(solution)/shard_map/ppermute | solution.py:291
  3.3 5.9 %collective-permute-start.1 = (f32[72,128]{1,0:T(8,128)S(1)}, f32[72,128]{1,0:T(8,128)S(1)}, u32[]{:S(2)}, u32[]{:S(2)}) collective-permute-start(f32[72,128]{1,0:T(8,128)S(1)} %again.1), channel_id=1, source_target_pairs={{0,1},{1,0},{2,3},{3,2},{4,5},{5,4},{6,7},{7,6},{8,9},{9,8},{10,11... | collective-permute-start | bytes 110600 | tf_op jit(solution)/shard_map/ppermute | solution.py:291
  9.3 5.0 %collective-permute-start.2 = (f32[8,896]{1,0:T(8,128)S(1)}, f32[8,896]{1,0:T(8,128)S(1)}, u32[]{:S(2)}, u32[]{:S(2)}) collective-permute-start(f32[8,896]{1,0:T(8,128)S(1)} %get-tuple-element.16), channel_id=1, source_target_pairs={{0,64},{1,65},{2,66},{3,67},{4,68},{5,69},{6,70},{7,71},{8,72},{9,... | collective-permute-start | bytes 86024 | tf_op jit(solution)/shard_map/ppermute | solution.py:291
  9.5 4.7 %collective-permute-start.3 = (f32[8,896]{1,0:T(8,128)S(1)}, f32[8,896]{1,0:T(8,128)S(1)}, u32[]{:S(2)}, u32[]{:S(2)}) collective-permute-start(f32[8,896]{1,0:T(8,128)S(1)} %get-tuple-element.17), channel_id=1, source_target_pairs={{0,1},{1,0},{2,3},{3,2},{4,5},{5,4},{6,7},{7,6},{8,9},{9,8},{10,11... | collective-permute-start | bytes 86024 | tf_op jit(solution)/shard_map/ppermute | solution.py:291

commit v3 on v2

--- a/solution.py
+++ b/solution.py
@@ -14,7 +14,7 @@
 BF16 = jnp.bfloat16
 NT = (((1,), (1,)), ((), ()))
 SCALE = 1.0 / 81.0
-LATE = 16
+LATE = 40
 VMEM = pl.BlockSpec(memory_space=pltpu.VMEM)
 HBM = pl.BlockSpec(memory_space=pl.ANY)
 
@@ -71,35 +71,41 @@
     return far, jnp.concatenate(right, axis=0), jnp.concatenate(left, axis=0)
 
 
-def pack_kernel(both, out, images):
+def pack_kernel(both, out, images, ready, edges, rr, lr, ring):
     images[...] = both[...]
     lane = iota((8, 128), 1)
-    edges = jnp.zeros((8, 128), F32)
+    sides = jnp.zeros((8, 128), F32)
     for g in range(ROWS // 8):
-        l0, l1, r0, r1 = [images[8 * g : 8 * g + 8, 128 * t : 128 * t + 128] for t in range(4)]
+        l0, l1, r0, r1 = [both[8 * g : 8 * g + 8, 128 * t : 128 * t + 128] for t in range(4)]
         out[8 * g : 8 * g + 8, :] = r1
         left = turn(jnp.where(lane >= 124, l1, l0), -8)
         some = jnp.where(lane < 4, r0, jnp.where(lane < 12, left, turn(r0, -16)))
-        edges = jnp.where(lane // 16 == g, turn(some, -16 * g), edges)
-    out[ROWS:, :] = edges
+        sides = jnp.where(lane // 16 == g, turn(some, -16 * g), sides)
+    out[ROWS:, :] = sides
+
+    @pl.when(waits_long())
+    def _():
+        inner(both, ready, edges, rr, lr, ring)
 
 
 def copy_kernel(x, out):
     out[...] = x[...]
 
 
-def rows_kernel(images, cross, intra, out1, out2):
-    odd = (lax.axis_index("row") % 2) == 1
+def rows_kernel(images, cross, intra, *sends):
+    row = lax.axis_index("row")
     west, east = neighbours(cross[...], intra[...])
-
-    def strip(g):
+    low = iota((8, 128), 0) < 4
+
+    def strip(g, mine):
         far, right_edge, left_edge = side_tiles(west, east, [g])
-        rows = images[8 * g : 8 * g + 8, :]
-        return jnp.concatenate([right_edge, far, rows[:, 256:512], left_edge, rows[:, 0:256]], axis=1)
-
-    top, bottom = strip(0), strip(ROWS // 8 - 1)
-    out1[...] = jnp.where(odd, top, bottom)
-    out2[...] = jnp.where(odd, bottom, top)
+        l0, l1, r0, r1 = [images[8 * g : 8 * g + 8, 128 * t : 128 * t + 128] for t in range(4)]
+        pairs = [(right_edge, left_edge), (far, l0), (r0, l1), (r1, l1)]
+        return jnp.concatenate([jnp.where(mine, r, pltpu.roll(l, 4, 0)) for r, l in pairs], axis=1)
+
+    top, bottom = strip(0, low), strip(ROWS // 8 - 1, ~low)
+    for boundary, send in enumerate(sends):
+        send[...] = jnp.where(row == boundary, bottom, top)
 
 
 def window(tiles, start):
@@ -166,7 +172,7 @@
     return pltpu.make_async_copy(blocks, blocks, sem)
 
 
-def inner_kernel(images, ready, edges, rr, lr, ring):
+def inner(images, ready, edges, rr, lr, ring):
     l0, l1, r0, r1 = [tile(images, t) for t in range(4)]
     bases, n = INNER
     lay_out([r0, r0, r0, r1, r1], [l0, l0, l1, l1], bases, n, rr, lr)
@@ -177,6 +183,19 @@
             ready[2 * k + h] = done[64 * h + 8 : 64 * h + 64]
 
     sweep(rr, lr, ring, own_band(), bases, n, emit)
+
+
+def waits_long():
+    c = lax.axis_index("col")
+    return (c % 16 == 1) & (c > 1)
+
+
+def inner_kernel(images, begun, part, ready, edges, rr, lr, ring):
+    del begun, part
+
+    @pl.when(~waits_long())
+    def _():
+        inner(images, ready, edges, rr, lr, ring)
 
 
 def outer_kernel(images, cross, intra, ready, part, out, late, edges, rr, lr, rr2, lr2, ring, ob, sem):
@@ -224,20 +243,18 @@
             store(r, 8 * u, tmp[pl.ds((size + 1) * 8 * u + r, 8, stride=size + 1), :])
 
 
-def edge_kernel(x1, x2, partial, late, alias, out, rr, lr, ring, ob, tmp, sem):
+def edge_kernel(x1, x2, x3, partial, late, alias, out, rr, lr, ring, ob, tmp, sem):
     del alias
     shipped = ship(late, out, SECOND, sem.at[0])
     row = lax.axis_index("row")
-    odd = (row % 2) == 1
     last = lax.axis_index("col") == lax.axis_size("col") - 1
-    north = jnp.where(odd, x1[...], x2[...])
-    south = jnp.where(odd, x2[...], x1[...])
-    north = jnp.where(row == 0, 0.0, north)
-    south = jnp.where(row == lax.axis_size("row") - 1, 0.0, south)
-    both = jnp.where(iota((8, 896), 0) >= 4, north, south)
-    parts = [both[:, 128 * t : 128 * t + 128] for t in range(7)]
-    right = [parts[0], parts[1], parts[2], parts[3], parts[0]]
-    left = [parts[4], parts[5], parts[6], parts[4]]
+    north = jnp.where(row == 1, x1[...], jnp.where(row == 2, x2[...], jnp.where(row == 3, x3[...], 0.0)))
+    south = jnp.where(row == 0, x1[...], jnp.where(row == 1, x2[...], jnp.where(row == 2, x3[...], 0.0)))
+    low = iota((8, 512), 0) < 4
+    right = jnp.where(low, south, north)
+    left = pltpu.roll(jnp.where(low, north, south), 4, 0)
+    right = [right[:, 128 * t : 128 * t + 128] for t in (0, 1, 2, 3, 0)]
+    left = [left[:, 128 * t : 128 * t + 128] for t in (0, 1, 2, 0)]
     bases = [16 * t for t in range(16)]
     lay_out(right, left, bases, 16, rr, lr)
     a, b = iota((128, 128), 0), iota((128, 128), 1)
@@ -300,62 +317,60 @@
     return r, c ^ 1
 
 
-def rows_even(r, c, rows, cols):
-    return r ^ 1, c
-
-
-def rows_odd(r, c, rows, cols):
-    s = r + 1 if r % 2 else r - 1
-    return (s, c) if 0 <= s < rows else (r, c ^ 1)
+def boundary_pairs(boundary):
+    other = {boundary: boundary + 1, boundary + 1: boundary}
+    return lambda r, c, rows, cols: (other[r], c) if r in other else (r, c ^ 1)
 
 
 def per_device(left, right):
     shape = jax.ShapeDtypeStruct
-    packed, images = pl.pallas_call(
+    volume = shape((ROWS, COLS, ND), F32)
+    sides = shape((COLS, 8, ND), F32)
+
+    def blocks(cols):
+        return shape((len(cols), ROWS - 8, ND), F32)
+
+    def scratch(*counts):
+        sizes = [size for n in counts for size in (n + 135, n + 8)]
+        return [pltpu.VMEM((-(-size // 8) * 8, 128), F32) for size in sizes] + [pltpu.VMEM((16, 128, 128), F32)]
+
+    def cost(cols):
+        return pl.CostEstimate(
+            flops=2 * 128 * 128 * 128 * len(cols), bytes_accessed=len(cols) << 15, transcendentals=0
+        )
+
+    packed, images, ready, edges = pl.pallas_call(
         pack_kernel,
         in_specs=[VMEM],
-        out_specs=[VMEM] * 2,
-        out_shape=[shape((ROWS + 8, 128), F32), shape((ROWS, 2 * COLS), F32)],
-        compiler_params=params(1),
+        out_specs=[VMEM] * 4,
+        out_shape=[shape((ROWS + 8, 128), F32), shape((ROWS, 2 * COLS), F32), blocks(BEFORE), sides],
+        scratch_shapes=scratch(INNER[1]),
+        compiler_params=params(4),
         name="pack",
     )(jnp.concatenate([left, right], axis=1))
     cross = exchange(packed, across)
     intra = exchange(pl.pallas_call(copy_kernel, in_specs=[VMEM], out_specs=VMEM, out_shape=shape((ROWS + 8, 128), F32), compiler_params=params(1), name="again")(packed), within)
-    volume = shape((ROWS, COLS, ND), F32)
-    sides = shape((COLS, 8, ND), F32)
-
-    def blocks(cols):
-        return shape((len(cols), ROWS - 8, ND), F32)
-
-    def scratch(*counts):
-        sizes = [size for n in counts for size in (n + 135, n + 8)]
-        return [pltpu.VMEM((-(-size // 8) * 8, 128), F32) for size in sizes] + [pltpu.VMEM((16, 128, 128), F32)]
-
-    def cost(cols):
-        return pl.CostEstimate(
-            flops=2 * 128 * 128 * 128 * len(cols), bytes_accessed=len(cols) << 15, transcendentals=0
-        )
-
     ready, edges = pl.pallas_call(
         inner_kernel,
-        in_specs=[VMEM],
+        in_specs=[VMEM] * 3,
         out_specs=[VMEM] * 2,
         out_shape=[blocks(BEFORE), sides],
         scratch_shapes=scratch(INNER[1]),
+        input_output_aliases={1: 0, 2: 1},
         compiler_params=params(4),
         cost_estimate=cost(BEFORE),
         name="inner",
-    )(images)
-    send1, send2 = pl.pallas_call(
+    )(images, ready, edges)
+    strip = shape((8, 512), F32)
+    sends = pl.pallas_call(
         rows_kernel,
         in_specs=[VMEM] * 3,
-        out_specs=[VMEM] * 2,
-        out_shape=[shape((8, 896), F32)] * 2,
+        out_specs=[VMEM] * 3,
+        out_shape=[strip] * 3,
         compiler_params=params(1),
         name="pack_rows",
     )(images, cross, intra)
-    got1 = exchange(send1, rows_even)
-    got2 = exchange(send2, rows_odd)
+    strips = [exchange(send, boundary_pairs(b)) for b, send in enumerate(sends)]
     out, late, edges = pl.pallas_call(
         outer_kernel,
         in_specs=[VMEM] * 5,
@@ -370,7 +385,7 @@
     )(images, cross, intra, ready, edges)
     return pl.pallas_call(
         edge_kernel,
-        in_specs=[VMEM, VMEM, VMEM, VMEM, HBM],
+        in_specs=[VMEM] * 5 + [HBM],
         out_specs=HBM,
         out_shape=volume,
         scratch_shapes=scratch(16)
@@ -379,10 +394,10 @@
             pltpu.VMEM((2, 8 * 129, 128), F32),
             pltpu.SemaphoreType.DMA((5,)),
         ],
-        input_output_aliases={4: 0},
+        input_output_aliases={5: 0},
         compiler_params=params(6),
         name="edge",
-    )(got1, got2, edges, late, out)
+    )(*strips, edges, late, out)
 
 
 def solution(mesh):

time: 16.2 us -> 15.4 us (0.951)
  starting transfers between devices: 8.34 us -> 6.96 us
  waiting for transfers between devices: 0.01 us -> 0.87 us
  Pallas kernels: 6.8 us -> 6.41 us
    ppermute x4 -> x5, starting transfers between devices: 8.34 us -> 6.96 us  [exchange(): return lax.ppermute(x, ('row', 'col'), pairs)]
    ppermute x4 -> x5, waiting for transfers between devices: 0.01 us -> 0.87 us  [exchange(): return lax.ppermute(x, ('row', 'col'), pairs)]
    pallas_call x1, Pallas kernels: 2.8 us -> 2.4 us  [per_device(): pl.pallas_call(outer_kernel, in_specs=[VMEM] * 5, out_specs=[HBM, VMEM, V...]
  transfers between devices with their start and end apart: 4 -> 5, of which waited for: 0 -> 1; matrix products, arithmetic and copies ran while one was open for 0% -> 0% of each run, Pallas kernels for 29% -> 16%
where the time goes in v3:
time: 15.4 us; the launch traced here: 15.2 us
  starting transfers between devices  6.96 us (45%)
  Pallas kernels  6.41 us (42%)
  other arithmetic  0.88 us (6%)
  waiting for transfers between devices  0.87 us (6%)
    ppermute x5, starting transfers between devices, exchange(): return lax.ppermute(x, ('row', 'col'), pairs)  6.96 us
    pallas_call x1, Pallas kernels, per_device(): pl.pallas_call(outer_kernel, in_specs=[VMEM] * 5, out_specs=[HBM, VMEM, V...  2.4 us
    pallas_call x1, Pallas kernels, per_device(): pl.pallas_call(pack_kernel, in_specs=[VMEM], out_specs=[VMEM] * 4, out_sh...  2.08 us
    pallas_call x1, Pallas kernels, per_device(): pl.pallas_call(edge_kernel, in_specs=[VMEM] * 5 + [HBM], out_specs=HBM, o...  1.83 us
    concatenate x1, other arithmetic, per_device(): jnp.concatenate([left, right], axis=1)  0.88 us
    ppermute x5, waiting for transfers between devices, exchange(): return lax.ppermute(x, ('row', 'col'), pairs)  0.87 us
  transfers between devices with their start and end apart: 5, of which 1 were waited for; matrix products, arithmetic and copies ran while one was open for 0% of the time, Pallas kernels for 16%

profile of v3, /device:TPU:27, one launch (start us, length us, event | category | flops | bytes accessed | tf_op | source)
XLA Modules:
  0.0 15.2 jit_solution(11864997949759772040)
XLA Ops:
  0.0 0.9 %pad_maximum_fusion.both = f32[64,512]{1,0:T(8,128)S(1)} fusion(f32[64,256]{1,0:T(8,128)} %param.3, f32[64,256]{1,0:T(8,128)} %param.2), kind=kLoop, calls=%fused_computation | loop fusion | flops 32768 | bytes 262144 | tf_op jit(solution)/shard_map/concatenate | solution.py:350
  0.9 2.1 %pack.1 = (f32[72,128]{1,0:T(8,128)S(1)}, f32[64,512]{1,0:T(8,128)S(1)}, f32[120,56,128]{2,1,0:T(8,128)S(1)}, f32[256,8,128]{2,1,0:T(8,128)S(1)}) custom-call(f32[64,512]{1,0:T(8,128)S(1)} %pad_maximum_fusion.both), custom_call_target="tpu_custom_call" | custom-call | tf_op jit(solution)/shard_map/pack/pallas_call | solution.py:342
  3.0 0.3 %collective-permute-start = (f32[72,128]{1,0:T(8,128)S(1)}, f32[72,128]{1,0:T(8,128)S(1)}, u32[]{:S(2)}, u32[]{:S(2)}) collective-permute-start(f32[72,128]{1,0:T(8,128)S(1)} %get-tuple-element.18.x), channel_id=1, source_target_pairs={{0,64},{1,2},{2,1},{3,4},{4,3},{5,6},{6,5},{7,8},{8,7},{9,10},{10,... | collective-permute-start | bytes 110600 | tf_op jit(solution)/shard_map/ppermute | solution.py:308
  3.3 4.0 %collective-permute-start.1 = (f32[72,128]{1,0:T(8,128)S(1)}, f32[72,128]{1,0:T(8,128)S(1)}, u32[]{:S(2)}, u32[]{:S(2)}) collective-permute-start(f32[72,128]{1,0:T(8,128)S(1)} %again.1), channel_id=1, source_target_pairs={{0,1},{1,0},{2,3},{3,2},{4,5},{5,4},{6,7},{7,6},{8,9},{9,8},{10,11... | collective-permute-start | bytes 110600 | tf_op jit(solution)/shard_map/ppermute | solution.py:308
  7.2 0.9 %collective-permute-done.1.intra = f32[72,128]{1,0:T(8,128)S(1)} collective-permute-done((f32[72,128]{1,0:T(8,128)S(1)}, f32[72,128]{1,0:T(8,128)S(1)}, u32[]{:S(2)}, u32[]{:S(2)}) %collective-permute-start.1) | collective-permute-done | bytes 36896 | tf_op jit(solution)/shard_map/ppermute | solution.py:308
  8.1 0.0 collective-permute-done.cross
  8.1 0.1 pack_rows.1
  8.2 0.3 %collective-permute-start.2 = (f32[8,512]{1,0:T(8,128)S(1)}, f32[8,512]{1,0:T(8,128)S(1)}, u32[]{:S(2)}, u32[]{:S(2)}) collective-permute-start(f32[8,512]{1,0:T(8,128)S(1)} %get-tuple-element.19), channel_id=1, source_target_pairs={{0,64},{1,65},{2,66},{3,67},{4,68},{5,69},{6,70},{7,71},{8,72},{9,... | collective-permute-start | bytes 49160 | tf_op jit(solution)/shard_map/ppermute | solution.py:308
  8.5 2.1 %collective-permute-start.3 = (f32[8,512]{1,0:T(8,128)S(1)}, f32[8,512]{1,0:T(8,128)S(1)}, u32[]{:S(2)}, u32[]{:S(2)}) collective-permute-start(f32[8,512]{1,0:T(8,128)S(1)} %get-tuple-element.20), channel_id=1, source_target_pairs={{0,1},{1,0},{2,3},{3,2},{4,5},{5,4},{6,7},{7,6},{8,9},{9,8},{10,11... | collective-permute-start | bytes 49160 | tf_op jit(solution)/shard_map/ppermute | solution.py:308
  10.5 0.4 %collective-permute-start.4 = (f32[8,512]{1,0:T(8,128)S(1)}, f32[8,512]{1,0:T(8,128)S(1)}, u32[]{:S(2)}, u32[]{:S(2)}) collective-permute-start(f32[8,512]{1,0:T(8,128)S(1)} %get-tuple-element.21), channel_id=1, source_target_pairs={{0,1},{1,0},{2,3},{3,2},{4,5},{5,4},{6,7},{7,6},{8,9},{9,8},{10,11... | collective-permute-start | bytes 49160 | tf_op jit(solution)/shard_map/ppermute | solution.py:308
  10.9 2.4 %outer.1 = (f32[64,256,128]{2,1,0:T(8,128)}, f32[80,56,128]{2,1,0:T(8,128)S(1)}, f32[256,8,128]{2,1,0:T(8,128)S(1)}) custom-call(f32[64,512]{1,0:T(8,128)S(1)} %get-tuple-element.17.images, f32[72,128]{1,0:T(8,128)S(1)} %collective-permute-done.cross, f32[72,128]{1,0:T(8,128)S(1)} %collective-permute-done.1.intra, ...), custom_call_target="tpu_custom_call", output_to_operand_aliasing={{2}: (4, {})} | custom-call | flops 570425344 | bytes 4456448 | tf_op jit(solution)/shard_map/outer/pallas_call | solution.py:374
  13.3 0.0 collective-permute-done.2.x1
  13.3 0.0 collective-permute-done.3.x2
  13.3 0.0 collective-permute-done.4.x3
  13.3 1.8 %edge.1 = f32[64,256,128]{2,1,0:T(8,128)} custom-call(f32[8,512]{1,0:T(8,128)S(1)} %collective-permute-done.2.x1, f32[8,512]{1,0:T(8,128)S(1)} %collective-permute-done.3.x2, f32[8,512]{1,0:T(8,128)S(1)} %collective-permute-done.4.x3, f32[256,8,128]{2,1,0:T(8,128)S(1)} %get-tuple-element.26.partial, ...), custom_call_target="tpu_custom_call", output_to_operand_aliasing={{}: (5, {})} | custom-call | tf_op jit(solution)/shard_map/edge/pallas_call | solution.py:386
  (2 shorter events, 0.0 us)
Async XLA Ops:
  3.0 5.1 %collective-permute-start = (f32[72,128]{1,0:T(8,128)S(1)}, f32[72,128]{1,0:T(8,128)S(1)}, u32[]{:S(2)}, u32[]{:S(2)}) collective-permute-start(f32[72,128]{1,0:T(8,128)S(1)} %get-tuple-element.18.x), channel_id=1, source_target_pairs={{0,64},{1,2},{2,1},{3,4},{4,3},{5,6},{6,5},{7,8},{8,7},{9,10},{10,... | collective-permute-start | bytes 110600 | tf_op jit(solution)/shard_map/ppermute | solution.py:308
  3.3 4.8 %collective-permute-start.1 = (f32[72,128]{1,0:T(8,128)S(1)}, f32[72,128]{1,0:T(8,128)S(1)}, u32[]{:S(2)}, u32[]{:S(2)}) collective-permute-start(f32[72,128]{1,0:T(8,128)S(1)} %again.1), channel_id=1, source_target_pairs={{0,1},{1,0},{2,3},{3,2},{4,5},{5,4},{6,7},{7,6},{8,9},{9,8},{10,11... | collective-permute-start | bytes 110600 | tf_op jit(solution)/shard_map/ppermute | solution.py:308
  8.2 5.1 %collective-permute-start.2 = (f32[8,512]{1,0:T(8,128)S(1)}, f32[8,512]{1,0:T(8,128)S(1)}, u32[]{:S(2)}, u32[]{:S(2)}) collective-permute-start(f32[8,512]{1,0:T(8,128)S(1)} %get-tuple-element.19), channel_id=1, source_target_pairs={{0,64},{1,65},{2,66},{3,67},{4,68},{5,69},{6,70},{7,71},{8,72},{9,... | collective-permute-start | bytes 49160 | tf_op jit(solution)/shard_map/ppermute | solution.py:308
  8.5 4.8 %collective-permute-start.3 = (f32[8,512]{1,0:T(8,128)S(1)}, f32[8,512]{1,0:T(8,128)S(1)}, u32[]{:S(2)}, u32[]{:S(2)}) collective-permute-start(f32[8,512]{1,0:T(8,128)S(1)} %get-tuple-element.20), channel_id=1, source_target_pairs={{0,1},{1,0},{2,3},{3,2},{4,5},{5,4},{6,7},{7,6},{8,9},{9,8},{10,11... | collective-permute-start | bytes 49160 | tf_op jit(solution)/shard_map/ppermute | solution.py:308
  10.5 2.8 %collective-permute-start.4 = (f32[8,512]{1,0:T(8,128)S(1)}, f32[8,512]{1,0:T(8,128)S(1)}, u32[]{:S(2)}, u32[]{:S(2)}) collective-permute-start(f32[8,512]{1,0:T(8,128)S(1)} %get-tuple-element.21), channel_id=1, source_target_pairs={{0,1},{1,0},{2,3},{3,2},{4,5},{5,4},{6,7},{7,6},{8,9},{9,8},{10,11... | collective-permute-start | bytes 49160 | tf_op jit(solution)/shard_map/ppermute | solution.py:308

commit v4 on v3

--- a/solution.py
+++ b/solution.py
@@ -391,7 +391,7 @@
         scratch_shapes=scratch(16)
         + [
             pltpu.VMEM((8, COLS, ND), F32),
-            pltpu.VMEM((2, 8 * 129, 128), F32),
+            pltpu.VMEM((2, 9 * 129, 128), F32),
             pltpu.SemaphoreType.DMA((5,)),
         ],
         input_output_aliases={5: 0},

time: 15.4 us -> 15.4 us (level)
  no operation moved by 1% of the time
where the time goes in v4:
time: 15.4 us; the launch traced here: 15.2 us
  starting transfers between devices  6.96 us (45%)
  Pallas kernels  6.4 us (42%)
  other arithmetic  0.88 us (6%)
  waiting for transfers between devices  0.87 us (6%)
    ppermute x5, starting transfers between devices, exchange(): return lax.ppermute(x, ('row', 'col'), pairs)  6.96 us
    pallas_call x1, Pallas kernels, per_device(): pl.pallas_call(outer_kernel, in_specs=[VMEM] * 5, out_specs=[HBM, VMEM, V...  2.4 us
    pallas_call x1, Pallas kernels, per_device(): pl.pallas_call(pack_kernel, in_specs=[VMEM], out_specs=[VMEM] * 4, out_sh...  2.08 us
    pallas_call x1, Pallas kernels, per_device(): pl.pallas_call(edge_kernel, in_specs=[VMEM] * 5 + [HBM], out_specs=HBM, o...  1.83 us
    concatenate x1, other arithmetic, per_device(): jnp.concatenate([left, right], axis=1)  0.88 us
    ppermute x5, waiting for transfers between devices, exchange(): return lax.ppermute(x, ('row', 'col'), pairs)  0.87 us
  transfers between devices with their start and end apart: 5, of which 1 were waited for; matrix products, arithmetic and copies ran while one was open for 0% of the time, Pallas kernels for 16%

profile of v4, /device:TPU:27, one launch (start us, length us, event | category | flops | bytes accessed | tf_op | source)
XLA Modules:
  0.0 15.2 jit_solution(5082916056617100475)
XLA Ops:
  0.0 0.9 %pad_maximum_fusion.both = f32[64,512]{1,0:T(8,128)S(1)} fusion(f32[64,256]{1,0:T(8,128)} %param.3, f32[64,256]{1,0:T(8,128)} %param.2), kind=kLoop, calls=%fused_computation | loop fusion | flops 32768 | bytes 262144 | tf_op jit(solution)/shard_map/concatenate | solution.py:350
  0.9 2.1 %pack.1 = (f32[72,128]{1,0:T(8,128)S(1)}, f32[64,512]{1,0:T(8,128)S(1)}, f32[120,56,128]{2,1,0:T(8,128)S(1)}, f32[256,8,128]{2,1,0:T(8,128)S(1)}) custom-call(f32[64,512]{1,0:T(8,128)S(1)} %pad_maximum_fusion.both), custom_call_target="tpu_custom_call" | custom-call | tf_op jit(solution)/shard_map/pack/pallas_call | solution.py:342
  3.0 0.3 %collective-permute-start = (f32[72,128]{1,0:T(8,128)S(1)}, f32[72,128]{1,0:T(8,128)S(1)}, u32[]{:S(2)}, u32[]{:S(2)}) collective-permute-start(f32[72,128]{1,0:T(8,128)S(1)} %get-tuple-element.18.x), channel_id=1, source_target_pairs={{0,64},{1,2},{2,1},{3,4},{4,3},{5,6},{6,5},{7,8},{8,7},{9,10},{10,... | collective-permute-start | bytes 110600 | tf_op jit(solution)/shard_map/ppermute | solution.py:308
  3.3 4.0 %collective-permute-start.1 = (f32[72,128]{1,0:T(8,128)S(1)}, f32[72,128]{1,0:T(8,128)S(1)}, u32[]{:S(2)}, u32[]{:S(2)}) collective-permute-start(f32[72,128]{1,0:T(8,128)S(1)} %again.1), channel_id=1, source_target_pairs={{0,1},{1,0},{2,3},{3,2},{4,5},{5,4},{6,7},{7,6},{8,9},{9,8},{10,11... | collective-permute-start | bytes 110600 | tf_op jit(solution)/shard_map/ppermute | solution.py:308
  7.2 0.9 %collective-permute-done.1.intra = f32[72,128]{1,0:T(8,128)S(1)} collective-permute-done((f32[72,128]{1,0:T(8,128)S(1)}, f32[72,128]{1,0:T(8,128)S(1)}, u32[]{:S(2)}, u32[]{:S(2)}) %collective-permute-start.1) | collective-permute-done | bytes 36896 | tf_op jit(solution)/shard_map/ppermute | solution.py:308
  8.1 0.0 collective-permute-done.cross
  8.1 0.1 pack_rows.1
  8.2 0.3 %collective-permute-start.2 = (f32[8,512]{1,0:T(8,128)S(1)}, f32[8,512]{1,0:T(8,128)S(1)}, u32[]{:S(2)}, u32[]{:S(2)}) collective-permute-start(f32[8,512]{1,0:T(8,128)S(1)} %get-tuple-element.19), channel_id=1, source_target_pairs={{0,64},{1,65},{2,66},{3,67},{4,68},{5,69},{6,70},{7,71},{8,72},{9,... | collective-permute-start | bytes 49160 | tf_op jit(solution)/shard_map/ppermute | solution.py:308
  8.5 2.1 %collective-permute-start.3 = (f32[8,512]{1,0:T(8,128)S(1)}, f32[8,512]{1,0:T(8,128)S(1)}, u32[]{:S(2)}, u32[]{:S(2)}) collective-permute-start(f32[8,512]{1,0:T(8,128)S(1)} %get-tuple-element.20), channel_id=1, source_target_pairs={{0,1},{1,0},{2,3},{3,2},{4,5},{5,4},{6,7},{7,6},{8,9},{9,8},{10,11... | collective-permute-start | bytes 49160 | tf_op jit(solution)/shard_map/ppermute | solution.py:308
  10.5 0.4 %collective-permute-start.4 = (f32[8,512]{1,0:T(8,128)S(1)}, f32[8,512]{1,0:T(8,128)S(1)}, u32[]{:S(2)}, u32[]{:S(2)}) collective-permute-start(f32[8,512]{1,0:T(8,128)S(1)} %get-tuple-element.21), channel_id=1, source_target_pairs={{0,1},{1,0},{2,3},{3,2},{4,5},{5,4},{6,7},{7,6},{8,9},{9,8},{10,11... | collective-permute-start | bytes 49160 | tf_op jit(solution)/shard_map/ppermute | solution.py:308
  10.9 2.4 %outer.1 = (f32[64,256,128]{2,1,0:T(8,128)}, f32[80,56,128]{2,1,0:T(8,128)S(1)}, f32[256,8,128]{2,1,0:T(8,128)S(1)}) custom-call(f32[64,512]{1,0:T(8,128)S(1)} %get-tuple-element.17.images, f32[72,128]{1,0:T(8,128)S(1)} %collective-permute-done.cross, f32[72,128]{1,0:T(8,128)S(1)} %collective-permute-done.1.intra, ...), custom_call_target="tpu_custom_call", output_to_operand_aliasing={{2}: (4, {})} | custom-call | flops 570425344 | bytes 4456448 | tf_op jit(solution)/shard_map/outer/pallas_call | solution.py:374
  13.3 0.0 collective-permute-done.2.x1
  13.3 0.0 collective-permute-done.3.x2
  13.3 0.0 collective-permute-done.4.x3
  13.3 1.8 %edge.1 = f32[64,256,128]{2,1,0:T(8,128)} custom-call(f32[8,512]{1,0:T(8,128)S(1)} %collective-permute-done.2.x1, f32[8,512]{1,0:T(8,128)S(1)} %collective-permute-done.3.x2, f32[8,512]{1,0:T(8,128)S(1)} %collective-permute-done.4.x3, f32[256,8,128]{2,1,0:T(8,128)S(1)} %get-tuple-element.26.partial, ...), custom_call_target="tpu_custom_call", output_to_operand_aliasing={{}: (5, {})} | custom-call | tf_op jit(solution)/shard_map/edge/pallas_call | solution.py:386
  (2 shorter events, 0.0 us)
Async XLA Ops:
  3.0 5.1 %collective-permute-start = (f32[72,128]{1,0:T(8,128)S(1)}, f32[72,128]{1,0:T(8,128)S(1)}, u32[]{:S(2)}, u32[]{:S(2)}) collective-permute-start(f32[72,128]{1,0:T(8,128)S(1)} %get-tuple-element.18.x), channel_id=1, source_target_pairs={{0,64},{1,2},{2,1},{3,4},{4,3},{5,6},{6,5},{7,8},{8,7},{9,10},{10,... | collective-permute-start | bytes 110600 | tf_op jit(solution)/shard_map/ppermute | solution.py:308
  3.3 4.8 %collective-permute-start.1 = (f32[72,128]{1,0:T(8,128)S(1)}, f32[72,128]{1,0:T(8,128)S(1)}, u32[]{:S(2)}, u32[]{:S(2)}) collective-permute-start(f32[72,128]{1,0:T(8,128)S(1)} %again.1), channel_id=1, source_target_pairs={{0,1},{1,0},{2,3},{3,2},{4,5},{5,4},{6,7},{7,6},{8,9},{9,8},{10,11... | collective-permute-start | bytes 110600 | tf_op jit(solution)/shard_map/ppermute | solution.py:308
  8.2 5.1 %collective-permute-start.2 = (f32[8,512]{1,0:T(8,128)S(1)}, f32[8,512]{1,0:T(8,128)S(1)}, u32[]{:S(2)}, u32[]{:S(2)}) collective-permute-start(f32[8,512]{1,0:T(8,128)S(1)} %get-tuple-element.19), channel_id=1, source_target_pairs={{0,64},{1,65},{2,66},{3,67},{4,68},{5,69},{6,70},{7,71},{8,72},{9,... | collective-permute-start | bytes 49160 | tf_op jit(solution)/shard_map/ppermute | solution.py:308
  8.5 4.8 %collective-permute-start.3 = (f32[8,512]{1,0:T(8,128)S(1)}, f32[8,512]{1,0:T(8,128)S(1)}, u32[]{:S(2)}, u32[]{:S(2)}) collective-permute-start(f32[8,512]{1,0:T(8,128)S(1)} %get-tuple-element.20), channel_id=1, source_target_pairs={{0,1},{1,0},{2,3},{3,2},{4,5},{5,4},{6,7},{7,6},{8,9},{9,8},{10,11... | collective-permute-start | bytes 49160 | tf_op jit(solution)/shard_map/ppermute | solution.py:308
  10.5 2.8 %collective-permute-start.4 = (f32[8,512]{1,0:T(8,128)S(1)}, f32[8,512]{1,0:T(8,128)S(1)}, u32[]{:S(2)}, u32[]{:S(2)}) collective-permute-start(f32[8,512]{1,0:T(8,128)S(1)} %get-tuple-element.21), channel_id=1, source_target_pairs={{0,1},{1,0},{2,3},{3,2},{4,5},{5,4},{6,7},{7,6},{8,9},{9,8},{10,11... | collective-permute-start | bytes 49160 | tf_op jit(solution)/shard_map/ppermute | solution.py:308

commit v5 on v4

--- a/solution.py
+++ b/solution.py
@@ -42,8 +42,8 @@
     rest = x - a.astype(F32)
     b = rest.astype(BF16)
     c = (rest - b.astype(F32)).astype(BF16)
-    dot = functools.partial(lax.dot_general, dimension_numbers=NT, preferred_element_type=F32)
-    return (dot(chosen, c) + dot(chosen, b)) + dot(chosen, a)
+    parts, picks = jnp.concatenate([c, b, a], axis=1), jnp.concatenate([chosen] * 3, axis=1)
+    return lax.dot_general(picks, parts, NT, preferred_element_type=F32)
 
 
 def neighbours(cross, intra):

time: 15.4 us -> 15.3 us (level)
    pallas_call x1, Pallas kernels: 2.08 us -> 1.91 us  [per_device(): pl.pallas_call(pack_kernel, in_specs=[VMEM], out_specs=[VMEM] * 4, out_sh...]
where the time goes in v5:
time: 15.3 us; the launch traced here: 15 us
  starting transfers between devices  6.98 us (46%)
  Pallas kernels  6.25 us (41%)
  other arithmetic  0.88 us (6%)
  waiting for transfers between devices  0.87 us (6%)
    ppermute x5, starting transfers between devices, exchange(): return lax.ppermute(x, ('row', 'col'), pairs)  6.98 us
    pallas_call x1, Pallas kernels, per_device(): pl.pallas_call(outer_kernel, in_specs=[VMEM] * 5, out_specs=[HBM, VMEM, V...  2.39 us
    pallas_call x1, Pallas kernels, per_device(): pl.pallas_call(pack_kernel, in_specs=[VMEM], out_specs=[VMEM] * 4, out_sh...  1.91 us
    pallas_call x1, Pallas kernels, per_device(): pl.pallas_call(edge_kernel, in_specs=[VMEM] * 5 + [HBM], out_specs=HBM, o...  1.86 us
    concatenate x1, other arithmetic, per_device(): jnp.concatenate([left, right], axis=1)  0.88 us
    ppermute x5, waiting for transfers between devices, exchange(): return lax.ppermute(x, ('row', 'col'), pairs)  0.87 us
  transfers between devices with their start and end apart: 5, of which 1 were waited for; matrix products, arithmetic and copies ran while one was open for 0% of the time, Pallas kernels for 16%

profile of v5, /device:TPU:27, one launch (start us, length us, event | category | flops | bytes accessed | tf_op | source)
XLA Modules:
  0.0 15.0 jit_solution(16402211166122000502)
XLA Ops:
  0.0 0.9 %pad_maximum_fusion.both = f32[64,512]{1,0:T(8,128)S(1)} fusion(f32[64,256]{1,0:T(8,128)} %param.3, f32[64,256]{1,0:T(8,128)} %param.2), kind=kLoop, calls=%fused_computation | loop fusion | flops 32768 | bytes 262144 | tf_op jit(solution)/shard_map/concatenate | solution.py:350
  0.9 1.9 %pack.1 = (f32[72,128]{1,0:T(8,128)S(1)}, f32[64,512]{1,0:T(8,128)S(1)}, f32[120,56,128]{2,1,0:T(8,128)S(1)}, f32[256,8,128]{2,1,0:T(8,128)S(1)}) custom-call(f32[64,512]{1,0:T(8,128)S(1)} %pad_maximum_fusion.both), custom_call_target="tpu_custom_call" | custom-call | tf_op jit(solution)/shard_map/pack/pallas_call | solution.py:342
  2.8 0.5 %collective-permute-start = (f32[72,128]{1,0:T(8,128)S(1)}, f32[72,128]{1,0:T(8,128)S(1)}, u32[]{:S(2)}, u32[]{:S(2)}) collective-permute-start(f32[72,128]{1,0:T(8,128)S(1)} %get-tuple-element.18.x), channel_id=1, source_target_pairs={{0,64},{1,2},{2,1},{3,4},{4,3},{5,6},{6,5},{7,8},{8,7},{9,10},{10,... | collective-permute-start | bytes 110600 | tf_op jit(solution)/shard_map/ppermute | solution.py:308
  3.3 4.0 %collective-permute-start.1 = (f32[72,128]{1,0:T(8,128)S(1)}, f32[72,128]{1,0:T(8,128)S(1)}, u32[]{:S(2)}, u32[]{:S(2)}) collective-permute-start(f32[72,128]{1,0:T(8,128)S(1)} %again.1), channel_id=1, source_target_pairs={{0,1},{1,0},{2,3},{3,2},{4,5},{5,4},{6,7},{7,6},{8,9},{9,8},{10,11... | collective-permute-start | bytes 110600 | tf_op jit(solution)/shard_map/ppermute | solution.py:308
  7.2 0.9 %collective-permute-done.1.intra = f32[72,128]{1,0:T(8,128)S(1)} collective-permute-done((f32[72,128]{1,0:T(8,128)S(1)}, f32[72,128]{1,0:T(8,128)S(1)}, u32[]{:S(2)}, u32[]{:S(2)}) %collective-permute-start.1) | collective-permute-done | bytes 36896 | tf_op jit(solution)/shard_map/ppermute | solution.py:308
  8.1 0.0 collective-permute-done.cross
  8.1 0.1 pack_rows.1
  8.2 0.3 %collective-permute-start.2 = (f32[8,512]{1,0:T(8,128)S(1)}, f32[8,512]{1,0:T(8,128)S(1)}, u32[]{:S(2)}, u32[]{:S(2)}) collective-permute-start(f32[8,512]{1,0:T(8,128)S(1)} %get-tuple-element.19), channel_id=1, source_target_pairs={{0,64},{1,65},{2,66},{3,67},{4,68},{5,69},{6,70},{7,71},{8,72},{9,... | collective-permute-start | bytes 49160 | tf_op jit(solution)/shard_map/ppermute | solution.py:308
  8.5 1.9 %collective-permute-start.3 = (f32[8,512]{1,0:T(8,128)S(1)}, f32[8,512]{1,0:T(8,128)S(1)}, u32[]{:S(2)}, u32[]{:S(2)}) collective-permute-start(f32[8,512]{1,0:T(8,128)S(1)} %get-tuple-element.20), channel_id=1, source_target_pairs={{0,1},{1,0},{2,3},{3,2},{4,5},{5,4},{6,7},{7,6},{8,9},{9,8},{10,11... | collective-permute-start | bytes 49160 | tf_op jit(solution)/shard_map/ppermute | solution.py:308
  10.4 0.4 %collective-permute-start.4 = (f32[8,512]{1,0:T(8,128)S(1)}, f32[8,512]{1,0:T(8,128)S(1)}, u32[]{:S(2)}, u32[]{:S(2)}) collective-permute-start(f32[8,512]{1,0:T(8,128)S(1)} %get-tuple-element.21), channel_id=1, source_target_pairs={{0,1},{1,0},{2,3},{3,2},{4,5},{5,4},{6,7},{7,6},{8,9},{9,8},{10,11... | collective-permute-start | bytes 49160 | tf_op jit(solution)/shard_map/ppermute | solution.py:308
  10.7 2.4 %outer.1 = (f32[64,256,128]{2,1,0:T(8,128)}, f32[80,56,128]{2,1,0:T(8,128)S(1)}, f32[256,8,128]{2,1,0:T(8,128)S(1)}) custom-call(f32[64,512]{1,0:T(8,128)S(1)} %get-tuple-element.17.images, f32[72,128]{1,0:T(8,128)S(1)} %collective-permute-done.cross, f32[72,128]{1,0:T(8,128)S(1)} %collective-permute-done.1.intra, ...), custom_call_target="tpu_custom_call", output_to_operand_aliasing={{2}: (4, {})} | custom-call | flops 570425344 | bytes 4456448 | tf_op jit(solution)/shard_map/outer/pallas_call | solution.py:374
  13.1 0.0 collective-permute-done.2.x1
  13.1 0.0 collective-permute-done.3.x2
  13.2 0.0 collective-permute-done.4.x3
  13.2 1.9 %edge.1 = f32[64,256,128]{2,1,0:T(8,128)} custom-call(f32[8,512]{1,0:T(8,128)S(1)} %collective-permute-done.2.x1, f32[8,512]{1,0:T(8,128)S(1)} %collective-permute-done.3.x2, f32[8,512]{1,0:T(8,128)S(1)} %collective-permute-done.4.x3, f32[256,8,128]{2,1,0:T(8,128)S(1)} %get-tuple-element.26.partial, ...), custom_call_target="tpu_custom_call", output_to_operand_aliasing={{}: (5, {})} | custom-call | tf_op jit(solution)/shard_map/edge/pallas_call | solution.py:386
  (2 shorter events, 0.0 us)
Async XLA Ops:
  2.8 5.3 %collective-permute-start = (f32[72,128]{1,0:T(8,128)S(1)}, f32[72,128]{1,0:T(8,128)S(1)}, u32[]{:S(2)}, u32[]{:S(2)}) collective-permute-start(f32[72,128]{1,0:T(8,128)S(1)} %get-tuple-element.18.x), channel_id=1, source_target_pairs={{0,64},{1,2},{2,1},{3,4},{4,3},{5,6},{6,5},{7,8},{8,7},{9,10},{10,... | collective-permute-start | bytes 110600 | tf_op jit(solution)/shard_map/ppermute | solution.py:308
  3.3 4.8 %collective-permute-start.1 = (f32[72,128]{1,0:T(8,128)S(1)}, f32[72,128]{1,0:T(8,128)S(1)}, u32[]{:S(2)}, u32[]{:S(2)}) collective-permute-start(f32[72,128]{1,0:T(8,128)S(1)} %again.1), channel_id=1, source_target_pairs={{0,1},{1,0},{2,3},{3,2},{4,5},{5,4},{6,7},{7,6},{8,9},{9,8},{10,11... | collective-permute-start | bytes 110600 | tf_op jit(solution)/shard_map/ppermute | solution.py:308
  8.2 4.9 %collective-permute-start.2 = (f32[8,512]{1,0:T(8,128)S(1)}, f32[8,512]{1,0:T(8,128)S(1)}, u32[]{:S(2)}, u32[]{:S(2)}) collective-permute-start(f32[8,512]{1,0:T(8,128)S(1)} %get-tuple-element.19), channel_id=1, source_target_pairs={{0,64},{1,65},{2,66},{3,67},{4,68},{5,69},{6,70},{7,71},{8,72},{9,... | collective-permute-start | bytes 49160 | tf_op jit(solution)/shard_map/ppermute | solution.py:308
  8.5 4.7 %collective-permute-start.3 = (f32[8,512]{1,0:T(8,128)S(1)}, f32[8,512]{1,0:T(8,128)S(1)}, u32[]{:S(2)}, u32[]{:S(2)}) collective-permute-start(f32[8,512]{1,0:T(8,128)S(1)} %get-tuple-element.20), channel_id=1, source_target_pairs={{0,1},{1,0},{2,3},{3,2},{4,5},{5,4},{6,7},{7,6},{8,9},{9,8},{10,11... | collective-permute-start | bytes 49160 | tf_op jit(solution)/shard_map/ppermute | solution.py:308
  10.4 2.8 %collective-permute-start.4 = (f32[8,512]{1,0:T(8,128)S(1)}, f32[8,512]{1,0:T(8,128)S(1)}, u32[]{:S(2)}, u32[]{:S(2)}) collective-permute-start(f32[8,512]{1,0:T(8,128)S(1)} %get-tuple-element.21), channel_id=1, source_target_pairs={{0,1},{1,0},{2,3},{3,2},{4,5},{5,4},{6,7},{7,6},{8,9},{9,8},{10,11... | collective-permute-start | bytes 49160 | tf_op jit(solution)/shard_map/ppermute | solution.py:308
